TPU v7x, 256 devices: a whole 4x4x8 slice. The times are simulated.
256 devices in a mesh: slab: 64 (over z, x, core), lvl: 4 (over y).
Axes of the slice: x: 4, y: 4, z: 8, core: 2. Of those that a mesh axis runs over, the one named last changes fastest.
Arguments:
- multipoles: bfloat16 [216, 524288], P(None, 'slab'), may hold values from -6 to 6
- fine_m2l: bfloat16 [16, 216, 216], P('lvl'), may hold values from -0.109375 to 0.109375
- m2m: bfloat16 [8, 216, 216], replicated, may hold values from -0.15625 to 0.15625
- coarse_m2l: bfloat16 [16, 216, 216], P('lvl'), may hold values from -0.109375 to 0.109375
- fine_source: int32 [16, 524288], P(None, 'slab'), may hold values from 0 to 12288
- ghost_index: int32 [2, 131072], replicated, may hold values from 0 to 8191
- ghost_count: int32 [2, 64], replicated, may hold values from 0 to 2048
- owner: int32 [65536, 1], P('slab'), may hold values from 0 to 63; in each aligned block of 1024 rows (0 to 1023, 1024 to 2047, ...) at most 32 rows name the same one
- coarse_source: int32 [16, 131072], P(None, 'slab'), may hold values from 0 to 2048
Outputs:
- fine_local: float32 [216, 524288], P(None, ('slab', 'lvl'))
- coarse_local: float32 [216, 131072], P(None, ('slab', 'lvl'))
Inputs may be any that keep to these rules, and one draw needn't show every extreme that they name: Among the 1024 parents of one slab, no owner is named more than 32 times, a bound that some block reaches.
All inputs are finite; a program needn't handle non-finite values.
Results may differ from a plain program's by a relative error of at most 0.0029.
Values may be sent and summed in bfloat16 or wider, within the bound.
No kernel may reach another device: no remote copies, remote signals or barrier semaphores. Data moves between devices by JAX's collectives and lax.ppermute only.
A program may use at most 128 MiB of HBM per device.

v0:
```python
import jax
import jax.numpy as jnp
from jax import lax
from jax.sharding import PartitionSpec as P

GHOST = 2048
PAR_DEV = 1024


def passed_along(block, axis, distance):
    devices = range(lax.axis_size(axis))
    route = [(i - distance, i) for i in devices if i - distance in devices]
    return lax.ppermute(block, axis, route)


def pack_ghosts(box_rows, ghost_index, ghost_count, target, direction_row):
    index_row = lax.dynamic_slice_in_dim(ghost_index[direction_row], target * GHOST, GHOST, 0)
    picked = jnp.take(box_rows, index_row, axis=0)
    inside = jnp.arange(GHOST, dtype=jnp.int32) < ghost_count[direction_row, target]
    return jnp.where(inside[:, None], picked, jnp.zeros_like(picked))


def stack_products(stack, sources, buffer_rows):
    op_count = stack.shape[0]
    coeffs = stack.shape[1]
    target_count = sources.shape[1]
    flat_ids = jnp.transpose(sources).reshape(-1)
    picked = jnp.take(buffer_rows, flat_ids, axis=0).reshape(target_count, op_count * coeffs)
    weights = jnp.transpose(stack, (1, 0, 2)).reshape(coeffs, op_count * coeffs)
    product = lax.dot_general(
        weights, picked, (((1,), (1,)), ((), ())), preferred_element_type=jnp.float32
    )
    return product


def per_device(
    multipoles,
    fine_m2l,
    m2m,
    coarse_m2l,
    fine_source,
    ghost_index,
    ghost_count,
    owner,
    coarse_source,
):
    coeffs = multipoles.shape[0]
    leaves = multipoles.shape[1]
    slab_count = lax.axis_size("slab")
    slab_here = lax.axis_index("slab")
    level_count = lax.axis_size("lvl")
    level_here = lax.axis_index("lvl")
    empty_row = jnp.zeros((1, coeffs), jnp.bfloat16)
    own_rows = jnp.transpose(multipoles)
    lower_block = passed_along(own_rows, "slab", 1)
    upper_block = passed_along(own_rows, "slab", -1)
    lower = pack_ghosts(lower_block, ghost_index, ghost_count, jnp.maximum(slab_here - 1, 0), 1)
    upper = pack_ghosts(
        upper_block, ghost_index, ghost_count, jnp.minimum(slab_here + 1, slab_count - 1), 0
    )
    buffer_rows = jnp.concatenate([own_rows, lower, upper, empty_row], axis=0)
    quarter = leaves // level_count
    targets = lax.dynamic_slice_in_dim(fine_source, level_here * quarter, quarter, 1)
    fine_local = stack_products(
        lax.all_gather(fine_m2l, "lvl", axis=0, tiled=True), targets, buffer_rows
    )
    parent_total = PAR_DEV
    children = multipoles.reshape(coeffs, parent_total, 8)
    parents = jnp.einsum("oij,jpo->ip", m2m, children, preferred_element_type=jnp.float32)
    parent_values = parents.astype(jnp.bfloat16)
    slot_count = coarse_source.shape[1]
    capacity = slot_count // slab_count
    owner_column = owner[:, 0]
    matches = (owner_column[:, None] == jnp.arange(slab_count, dtype=jnp.int32)[None, :]).astype(
        jnp.int32
    )
    before = jnp.cumsum(matches, axis=0) - matches
    slot_rank = jnp.sum(before * matches, axis=1)
    column = owner_column * capacity + slot_rank
    placing = (column[:, None] == jnp.arange(slot_count, dtype=jnp.int32)[None, :]).astype(
        jnp.bfloat16
    )
    outgoing = lax.dot_general(
        placing, parent_values, (((0,), (1,)), ((), ())), preferred_element_type=jnp.float32
    ).astype(jnp.bfloat16)
    received = lax.all_to_all(outgoing, "slab", split_axis=0, concat_axis=0, tiled=True)
    coarse_rows = jnp.concatenate([received, empty_row], axis=0)
    coarse_quarter = slot_count // level_count
    coarse_targets = lax.dynamic_slice_in_dim(
        coarse_source, level_here * coarse_quarter, coarse_quarter, 1
    )
    coarse_local = stack_products(
        lax.all_gather(coarse_m2l, "lvl", axis=0, tiled=True), coarse_targets, coarse_rows
    )
    return (fine_local, coarse_local)


def solution(mesh):
    placed = (
        P(None, "slab"),
        P("lvl", None, None),
        P(),
        P("lvl", None, None),
        P(None, "slab"),
        P(),
        P(),
        P("slab", None),
        P(None, "slab"),
    )
    return jax.shard_map(
        per_device,
        mesh=mesh,
        in_specs=placed,
        out_specs=(P(None, ("slab", "lvl")), P(None, ("slab", "lvl"))),
        check_vma=False,
    )
```

profile of v0, /device:TPU:1, one launch (start us, length us, event | category | flops | bytes accessed | tf_op | source)
XLA Modules:
  0.0 356.2 jit_solution(11195960094926564104)
XLA Ops:
  7.2 0.0 copy-start
  7.2 0.0 copy-start.3
  7.2 0.0 all-gather.5.cloned.1.call-start
  7.2 0.7 all-gather.5.cloned.1.call-update
  7.9 4.5 %collective-permute-start = (bf16[8192,216]{0,1:T(8,128)(2,1)}, bf16[8192,216]{0,1:T(8,128)(2,1)}, u32[]{:S(2)}, u32[]{:S(2)}) collective-permute-start(bf16[8192,216]{0,1:T(8,128)(2,1)} %bitcast.71), channel_id=1, source_target_pairs={{0,4},{4,8},{8,12},{12,16},{16,20},{20,24},{24,28},{28,32},{32,36}... | collective-permute-start | bytes 10616840 | tf_op jit(solution)/shard_map/ppermute | solution.py:13
  12.4 3.7 %collective-permute-start.1 = (bf16[8192,216]{0,1:T(8,128)(2,1)}, bf16[8192,216]{0,1:T(8,128)(2,1)}, u32[]{:S(2)}, u32[]{:S(2)}) collective-permute-start(bf16[8192,216]{0,1:T(8,128)(2,1)} %bitcast.72), channel_id=1, source_target_pairs={{4,0},{8,4},{12,8},{16,12},{20,16},{24,20},{28,24},{32,28},{36,32}... | collective-permute-start | bytes 10616840 | tf_op jit(solution)/shard_map/ppermute | solution.py:13
  16.2 6.2 %copy.24 = bf16[216,8192]{0,1:T(8,128)(2,1)} copy(bf16[216,8192]{1,0:T(8,128)(2,1)} %param.11) | data formatting | bytes 7077888 | tf_op args[0]
  22.4 18.0 %reduce-window.6 = s32[64,8,128]{2,1,0:T(8,128)S(1)} reduce-window(s32[64,8,128]{2,1,0:T(8,128)S(1)} %fusion.34, s32[]{:T(128)} %constant.38.clone.1), window={size=1x1x128 pad=0_0x0_0x127_0}, to_apply=%region_0.0 | reduce-window | flops 8323072 | bytes 524292 | tf_op jit(solution)/shard_map/reduce-window
  40.4 0.1 slice.24
  40.5 0.1 copy.31
  40.7 0.1 copy.32
  40.8 0.1 broadcast_add_fusion
  40.9 0.1 fusion.33
  41.0 5.4 %fusion.14 = bf16[2048,216]{0,1:T(8,128)(2,1)S(1)} fusion(s32[1024]{0:T(1024)S(1)} %bitcast.84, bf16[8,216,216]{2,1,0:T(8,128)(2,1)S(1)} %copy-done, bf16[216,1024,8]{0,2,1:T(8,128)(2,1)} %bitcast.67), kind=kOutput, calls=%fused_computation.18 | convolution fusion | flops 1673142272 | bytes 5174272 | tf_op jit(solution)/shard_map/dot_general | solution.py:83
  46.5 1.3 copy.35
  47.8 11.3 %all-to-all-start = ((bf16[64,32,216]{2,1,0:T(8,128)(2,1)}), bf16[64,32,216]{2,1,0:T(8,128)(2,1)S(1)}, u32[]{:S(2)}, u32[]{:S(2)}) async-start(bf16[64,32,216]{2,1,0:T(8,128)(2,1)} %bitcast.22), calls=%async_computation | async-start | bytes 2097152 | tf_op jit(solution)/shard_map/all_to_all | solution.py:86
  59.1 0.0 all-gather.3.cloned.1.call-start
  59.1 0.7 all-gather.3.cloned.1.call-update
  59.9 0.8 compare_and_fusion.1
  60.6 0.1 copy.36
  60.8 0.2 reshape.132
  60.9 1.0 compare_and_fusion
  61.9 0.3 copy.29
  62.2 0.4 reshape.129
  62.6 0.1 compare_select_fusion
  62.8 2.5 fusion.39
  65.3 0.0 copy-done.4
  65.3 0.6 constant_dynamic-slice_fusion.3
  65.9 0.7 iota_compare_fusion.7
  66.6 0.6 iota_compare_fusion.6
  67.3 19.8 %all-to-all-done = bf16[64,32,216]{2,1,0:T(8,128)(2,1)S(1)} async-done(((bf16[64,32,216]{2,1,0:T(8,128)(2,1)}), bf16[64,32,216]{2,1,0:T(8,128)(2,1)S(1)}, u32[]{:S(2)}, u32[]{:S(2)}) %all-to-all-start) | async-done | bytes 884768 | tf_op jit(solution)/shard_map/all_to_all | solution.py:86
  87.1 0.2 concatenate.7
  87.3 33.1 %gather_fusion.1 = bf16[8192,216]{1,0:T(8,128)(2,1)} fusion(bf16[2049,216]{1,0:T(8,128)(2,1)S(1)} %concatenate.7, s32[8192]{0:T(1024)S(1)} %broadcast_clamp_fusion.1), kind=kCustom, calls=%fused_computation.3 | custom fusion | bytes 7110656 | tf_op jit(solution)/shard_map/jit(_take)/gather | solution.py:28
  120.4 7.8 %copy.37 = bf16[512,16,216]{0,2,1:T(8,128)(2,1)} copy(bf16[512,16,216]{2,1,0:T(8,128)(2,1)} %bitcast.69) | data formatting | bytes 7077888 | tf_op jit(solution)/shard_map/jit(_take)/gather | solution.py:28
  128.2 4.3 %fusion.24 = f32[216,512]{1,0:T(8,128)} fusion(bf16[16,216,216]{2,1,0:T(8,128)(2,1)} %all-gather.5.cloned.1.call-done, bf16[512,16,216]{0,2,1:T(8,128)(2,1)} %copy.37, pred[512,16]{0,1:T(8,128)(4,1)S(1)} %get-tuple-element.3), kind=kOutput, calls=%fused_computation.24 | convolution fusion | flops 766181376 | bytes 5482496 | tf_op jit(solution)/shard_map/dot_general | solution.py:30
  132.6 0.0 collective-permute-done
  132.6 6.2 %copy.26 = bf16[8192,216]{1,0:T(8,128)(2,1)} copy(bf16[8192,216]{0,1:T(8,128)(2,1)} %collective-permute-done) | data formatting | bytes 7077888 | tf_op jit(solution)/shard_map/ppermute | solution.py:13
  138.8 9.4 %gather_fusion.2 = bf16[2048,216]{1,0:T(8,128)(2,1)S(1)} fusion(bf16[8192,216]{1,0:T(8,128)(2,1)} %copy.26, s32[2048]{0:T(1024)S(1)} %fusion.35), kind=kCustom, calls=%fused_computation.clone | custom fusion | bytes 1777664 | tf_op jit(solution)/shard_map/jit(_take)/gather | solution.py:18
  148.1 0.0 collective-permute-done.1
  148.2 6.2 %copy.28 = bf16[8192,216]{1,0:T(8,128)(2,1)} copy(bf16[8192,216]{0,1:T(8,128)(2,1)} %collective-permute-done.1) | data formatting | bytes 7077888 | tf_op jit(solution)/shard_map/ppermute | solution.py:13
  154.4 9.4 %gather_fusion.3 = bf16[2048,216]{1,0:T(8,128)(2,1)S(1)} fusion(bf16[8192,216]{1,0:T(8,128)(2,1)} %copy.28, s32[2048]{0:T(1024)S(1)} %fusion.36), kind=kCustom, calls=%fused_computation.1.clone | custom fusion | bytes 1777664 | tf_op jit(solution)/shard_map/jit(_take)/gather | solution.py:18
  163.8 1.5 select_select_fusion.1
  165.2 1.5 select_select_fusion
  166.7 0.0 copy-done.2
  166.7 24.6 %maximum_maximum_fusion = bf16[12289,216]{1,0:T(8,128)(2,1)} fusion(bf16[2048,216]{1,0:T(8,128)(2,1)S(1)} %select_select_fusion, bf16[2048,216]{1,0:T(8,128)(2,1)S(1)} %select_select_fusion.1, bf16[8192,216]{1,0:T(8,128)(2,1)S(1)} %bitcast.68, bf16[12289]{0:T(1024)(128)(2,1)S(1)} %pad.4.clone), kind=kLoop, calls=%fused_computation.10 | loop fusion | flops 21235392 | bytes 10641842 | tf_op jit(solution)/shard_map/concatenate | solution.py:61
  191.4 124.3 %gather_fusion = bf16[32768,216]{1,0:T(8,128)(2,1)} fusion(bf16[12289,216]{1,0:T(8,128)(2,1)} %maximum_maximum_fusion, s32[32768]{0:T(1024)S(1)} %broadcast_clamp_fusion), kind=kCustom, calls=%fused_computation.2 | custom fusion | bytes 28442624 | tf_op jit(solution)/shard_map/jit(_take)/gather | solution.py:28
  315.6 23.5 %copy.30 = bf16[2048,16,216]{0,2,1:T(8,128)(2,1)} copy(bf16[2048,16,216]{2,1,0:T(8,128)(2,1)} %bitcast.66) | data formatting | bytes 28311552 | tf_op jit(solution)/shard_map/jit(_take)/gather | solution.py:28
  339.1 10.2 %fusion.11 = f32[216,2048]{1,0:T(8,128)} fusion(bf16[2048,16,216]{0,2,1:T(8,128)(2,1)} %copy.30, pred[2048,16]{0,1:T(8,128)(4,1)S(1)} %get-tuple-element.5, bf16[16,216,216]{2,1,0:T(8,128)(2,1)} %all-gather.3.cloned.1.call-done), kind=kOutput, calls=%fused_computation.17 | convolution fusion | flops 3064725504 | bytes 17451008 | tf_op jit(solution)/shard_map/dot_general | solution.py:30
  (21 shorter events, 0.2 us)
Async XLA Ops:
  7.2 33.9 %copy-start = (bf16[8,216,216]{2,1,0:T(8,128)(2,1)S(1)}, bf16[8,216,216]{2,1,0:T(8,128)(2,1)}, u32[]{:S(2)}) copy-start(bf16[8,216,216]{2,1,0:T(8,128)(2,1)} %param.13) | copy-start | bytes 2239492
  7.2 15.2 %copy-start.3 = (s32[1024,1]{0,1:T(1,128)S(1)}, s32[1024,1]{0,1:T(1,128)}, u32[]{:S(2)}) copy-start(s32[1024,1]{0,1:T(1,128)} %param.18) | copy-start | bytes 12292
  7.2 121.0 %all-gather.5.cloned.1.call-start = ((), (), s32[]{:S(2)}) async-start(), calls=%async_computation.2 | async-start | bytes 2211840 | tf_op jit(solution)/shard_map/all_gather | solution.py:93
  7.9 124.6 %collective-permute-start = (bf16[8192,216]{0,1:T(8,128)(2,1)}, bf16[8192,216]{0,1:T(8,128)(2,1)}, u32[]{:S(2)}, u32[]{:S(2)}) collective-permute-start(bf16[8192,216]{0,1:T(8,128)(2,1)} %bitcast.71), channel_id=1, source_target_pairs={{0,4},{4,8},{8,12},{12,16},{16,20},{20,24},{24,28},{28,32},{32,36}... | collective-permute-start | bytes 10616840 | tf_op jit(solution)/shard_map/ppermute | solution.py:13
  12.4 135.7 %collective-permute-start.1 = (bf16[8192,216]{0,1:T(8,128)(2,1)}, bf16[8192,216]{0,1:T(8,128)(2,1)}, u32[]{:S(2)}, u32[]{:S(2)}) collective-permute-start(bf16[8192,216]{0,1:T(8,128)(2,1)} %bitcast.72), channel_id=1, source_target_pairs={{4,0},{8,4},{12,8},{16,12},{20,16},{24,20},{28,24},{32,28},{36,32}... | collective-permute-start | bytes 10616840 | tf_op jit(solution)/shard_map/ppermute | solution.py:13
  47.8 17.5 %copy-start.4 = (s32[2,64]{1,0:T(2,128)S(1)}, s32[2,64]{1,0:T(2,128)}, u32[]{:S(2)}) copy-start(s32[2,64]{1,0:T(2,128)} %param.17) | copy-start | bytes 1540
  47.8 39.3 %all-to-all-start = ((bf16[64,32,216]{2,1,0:T(8,128)(2,1)}), bf16[64,32,216]{2,1,0:T(8,128)(2,1)S(1)}, u32[]{:S(2)}, u32[]{:S(2)}) async-start(bf16[64,32,216]{2,1,0:T(8,128)(2,1)} %bitcast.22), calls=%async_computation | async-start | bytes 2097152 | tf_op jit(solution)/shard_map/all_to_all | solution.py:86
  59.1 280.1 %all-gather.3.cloned.1.call-start = ((), (), s32[]{:S(2)}) async-start(), calls=%async_computation.1 | async-start | bytes 2211840 | tf_op jit(solution)/shard_map/all_gather | solution.py:65
  163.7 3.0 copy-start.2
  339.1 10.2 %copy-start.1 = (bf16[8,216,216]{2,1,0:T(8,128)(2,1)S(1)}, bf16[8,216,216]{2,1,0:T(8,128)(2,1)}, u32[]{:S(2)}) copy-start(bf16[8,216,216]{2,1,0:T(8,128)(2,1)} %param.13) | copy-start | bytes 2239492
Sparse Core Ops, SparseCore 0:
  9.8 34.4 all-gather.4
  61.7 31.8 all-gather.2
where the time goes:
time: 358 us; the launch traced here: 356 us
  local copies, waits for them, and re-layouts  232 us (65%)
  other arithmetic  49 us (14%)
  waiting for transfers between devices  21.2 us (6%)
  matrix products  20 us (6%)
  starting transfers between devices  19.6 us (5%)
  between operations  14.4 us (4%)
    gather x4, local copies, waits for them, and re-layouts, stack_products(): jnp.take(buffer_rows, flat_ids, axis=0)  189 us
    concatenate x1, other arithmetic, per_device(): buffer_rows = jnp.concatenate([own_rows, lower, upper, empty_row], axis=0)  24.6 us
    all_to_all x1, waiting for transfers between devices, per_device(): lax.all_to_all(outgoing, 'slab', split_axis=0, concat_axis=0, tiled=True)  19.8 us
    gather x2, local copies, waits for them, and re-layouts, pack_ghosts(): picked = jnp.take(box_rows, index_row, axis=0)  18.7 us
    another operation x3, other arithmetic  18.2 us
    dot_general x2, matrix products, stack_products(): lax.dot_general(weights, picked, (((1,), (1,)), ((), ())), preferred_elem...  14.6 us
    ppermute x2, local copies, waits for them, and re-layouts, passed_along(): return lax.ppermute(block, axis, route)  12.4 us
    all_to_all x1, starting transfers between devices, per_device(): lax.all_to_all(outgoing, 'slab', split_axis=0, concat_axis=0, tiled=True)  11.3 us
  transfers between devices with their start and end apart: 5, of which 1 were waited for; matrix products, arithmetic and copies ran while one was open for 82% of the time, Pallas kernels for 0%

commit v1 on v0

v1 whole, which is shorter than its diff:
```python
import jax
import jax.numpy as jnp
from jax import lax
from jax.experimental import pallas as pl
from jax.experimental.pallas import tpu as pltpu
from jax.sharding import PartitionSpec as P

COEFFS = 216
LANES = 128
OPS = 16
TILE = 256
LEAVES = 8192
GHOST = 2048
PARENTS = 1024
SLOTS = 2048
TAIL = 16
BLOCK = 256
GROUP = 2048

ANY = pl.BlockSpec(memory_space=pl.ANY)
VMEM = pl.BlockSpec(memory_space=pltpu.VMEM)
SMEM = pl.BlockSpec(memory_space=pltpu.SMEM)


def contract_lanes(a, b):
    return lax.dot_general(a, b, (((1,), (1,)), ((), ())), preferred_element_type=jnp.float32)


def rows_body(picks, x, rows, sent, spread, stage, sem):
    r = lax.broadcasted_iota(jnp.int32, (2 * BLOCK, BLOCK), 0)
    c = lax.broadcasted_iota(jnp.int32, (2 * BLOCK, BLOCK), 1)
    for h in range(2):
        spread[h] = jnp.where(r == 2 * c + h, 1.0, 0.0).astype(jnp.bfloat16)
    flat = rows.reshape(2 * (LEAVES + TAIL), LANES)
    rows[pl.ds(LEAVES, TAIL)] = jnp.zeros((TAIL, 2, LANES), jnp.bfloat16)
    blocks = LEAVES // BLOCK

    def move(b):
        here = pl.ds(pl.multiple_of(b * 2 * BLOCK, 2 * BLOCK), 2 * BLOCK)
        return pltpu.make_async_copy(stage.at[here], flat.at[here], sem)

    @pl.loop(0, blocks)
    def _(b):
        cols = pl.ds(pl.multiple_of(b * BLOCK, BLOCK), BLOCK)
        low = contract_lanes(spread[0], x[0:LANES, cols])
        high = contract_lanes(spread[1], x[LANES:COEFFS, cols])
        high = jnp.concatenate([high, jnp.zeros((2 * BLOCK, 2 * LANES - COEFFS), jnp.float32)], axis=1)
        here = pl.ds(pl.multiple_of(b * 2 * BLOCK, 2 * BLOCK), 2 * BLOCK)
        stage[here] = (low + high).astype(jnp.bfloat16)

    whole = pltpu.make_async_copy(stage, flat.at[pl.ds(0, 2 * LEAVES)], sem)
    whole.start()
    whole.wait()
    for d in range(2):
        for g in range(GHOST):
            f = d * GHOST + g
            sent[d, g] = rows[picks[f // LANES, f % LANES]]


def leaf_rows(multipoles, picks):
    return pl.pallas_call(
        rows_body,
        name="leaf_rows",
        in_specs=[SMEM, VMEM],
        out_specs=[VMEM, VMEM],
        out_shape=[
            jax.ShapeDtypeStruct((LEAVES + TAIL, 2, LANES), jnp.bfloat16),
            jax.ShapeDtypeStruct((2, GHOST, 2, LANES), jnp.bfloat16),
        ],
        scratch_shapes=[
            pltpu.VMEM((2, 2 * BLOCK, BLOCK), jnp.bfloat16),
            pltpu.VMEM((2 * LEAVES, LANES), jnp.bfloat16),
            pltpu.SemaphoreType.DMA(()),
        ],
        compiler_params=pltpu.CompilerParams(vmem_limit_bytes=40 << 20),
        cost_estimate=pl.CostEstimate(flops=6_000_000_000, bytes_accessed=10 << 20, transcendentals=0),
    )(picks, multipoles)


def parents_body(place, x, w, out, children, pairs, stage, rows, sem):
    out[...] = jnp.zeros_like(out)
    per_block = BLOCK // 8
    r = lax.broadcasted_iota(jnp.int32, (BLOCK, BLOCK), 0)
    c = lax.broadcasted_iota(jnp.int32, (BLOCK, BLOCK), 1)
    octant_major = jnp.where(c == (r % per_block) * 8 + r // per_block, 1.0, 0.0).astype(jnp.bfloat16)
    per_group = GROUP // 8

    @pl.loop(0, LEAVES // GROUP)
    def _(s):
        for b in range(GROUP // BLOCK):
            cols = pl.ds(pl.multiple_of(s * GROUP + b * BLOCK, BLOCK), BLOCK)
            sorted_rows = contract_lanes(octant_major, x[:, cols]).astype(jnp.bfloat16)
            for o in range(8):
                children[o, b * per_block : (b + 1) * per_block] = sorted_rows[o * per_block : (o + 1) * per_block]
        total = jnp.dot(children[0], w[0], preferred_element_type=jnp.float32)
        for o in range(1, 8):
            total += jnp.dot(children[o], w[o], preferred_element_type=jnp.float32)
        pairs[pl.ds(0, per_group, 2), :] = total[:, :LANES]
        pairs[pl.ds(1, per_group, 2), :] = total[:, LANES:]
        here = pl.ds(pl.multiple_of(s * 2 * per_group, 2 * per_group), 2 * per_group)
        stage[here] = pairs[...].astype(jnp.bfloat16)

    move = pltpu.make_async_copy(stage, rows.reshape(2 * PARENTS, LANES), sem)
    move.start()
    move.wait()
    for p in range(PARENTS):
        out[place[p // LANES, p % LANES]] = rows[p]


def placed_parents(multipoles, weights, place):
    return pl.pallas_call(
        parents_body,
        name="placed_parents",
        in_specs=[SMEM, VMEM, VMEM],
        out_specs=VMEM,
        out_shape=jax.ShapeDtypeStruct((SLOTS, 2, LANES), jnp.bfloat16),
        scratch_shapes=[
            pltpu.VMEM((8, GROUP // 8, COEFFS), jnp.bfloat16),
            pltpu.VMEM((GROUP // 4, LANES), jnp.float32),
            pltpu.VMEM((2 * PARENTS, LANES), jnp.bfloat16),
            pltpu.VMEM((PARENTS, 2, LANES), jnp.bfloat16),
            pltpu.SemaphoreType.DMA(()),
        ],
        compiler_params=pltpu.CompilerParams(vmem_limit_bytes=40 << 20),
        cost_estimate=pl.CostEstimate(flops=4_000_000_000, bytes_accessed=6 << 20, transcendentals=0),
    )(place, multipoles, weights)


def translate(name, sources, weights, parts, slots, gflops):
    targets = sources.shape[1]
    tiles = targets // TILE
    n = len(parts)
    width = OPS * TILE // LANES
    src = sources.reshape(OPS, tiles, TILE).swapaxes(0, 1).reshape(tiles, width, LANES)

    def body(src_ref, w, *refs):
        part_refs = refs[:n]
        out = refs[n]
        buf, za, zb, zz, res, sa, sb, psem, isem, zsem = refs[n + 1 :]
        copies = [
            pltpu.make_async_copy(part_refs[k].at[pl.ds(first, rows)], buf.at[pl.ds(start, rows)], psem.at[k])
            for k, (_, start, first, rows) in enumerate(parts)
        ]
        for copy in copies:
            copy.start()

        def fetch(tile, dst, which):
            return pltpu.make_async_copy(src_ref.at[tile], dst, isem.at[which])

        fetch(0, sa, 0).start()
        fetch(1, sb, 1).start()
        for copy in copies:
            copy.wait()

        def gather(idx, z):
            for o in range(OPS):
                for u in range(TILE):
                    f = o * TILE + u
                    z[o, u] = buf[idx[f // LANES, f % LANES]]

        def multiply(z, tile):
            relaid = pltpu.make_async_copy(z.reshape(OPS, 2 * TILE, LANES), zz, zsem)
            relaid.start()
            relaid.wait()
            lhs = jnp.concatenate([zz[o] for o in range(OPS)], axis=1)
            for h in range(2):
                d = jnp.dot(lhs, w[:, h * 256 : (h + 1) * 256], preferred_element_type=jnp.float32)
                res[2 * h] = d[:, :LANES]
                res[2 * h + 1] = d[:, LANES:]
            cols = pl.ds(pl.multiple_of(tile * TILE, TILE), TILE)
            for c in range(2):
                total = res[c, pl.ds(0, TILE, 2), :] + res[2 + c, pl.ds(1, TILE, 2), :]
                rows = min(LANES, COEFFS - c * LANES)
                out[c * LANES : c * LANES + rows, cols] = total.T[:rows]

        @pl.loop(0, tiles // 2)
        def _(i):
            fetch(0, sa, 0).wait()
            gather(sa, za)
            multiply(za, 2 * i)

            @pl.when(i < tiles // 2 - 1)
            def _():
                fetch(2 * i + 2, sa, 0).start()

            fetch(0, sb, 1).wait()
            gather(sb, zb)
            multiply(zb, 2 * i + 1)

            @pl.when(i < tiles // 2 - 1)
            def _():
                fetch(2 * i + 3, sb, 1).start()

    return pl.pallas_call(
        body,
        name=name,
        in_specs=[ANY, VMEM] + [ANY] * n,
        out_specs=VMEM,
        out_shape=jax.ShapeDtypeStruct((COEFFS, targets), jnp.float32),
        scratch_shapes=[
            pltpu.VMEM((slots, 2, LANES), jnp.bfloat16),
            pltpu.VMEM((OPS, TILE, 2, LANES), jnp.bfloat16),
            pltpu.VMEM((OPS, TILE, 2, LANES), jnp.bfloat16),
            pltpu.VMEM((OPS, 2 * TILE, LANES), jnp.bfloat16),
            pltpu.VMEM((4, 2 * TILE, LANES), jnp.float32),
            pltpu.SMEM((width, LANES), jnp.int32),
            pltpu.SMEM((width, LANES), jnp.int32),
            pltpu.SemaphoreType.DMA((n,)),
            pltpu.SemaphoreType.DMA((2,)),
            pltpu.SemaphoreType.DMA(()),
        ],
        compiler_params=pltpu.CompilerParams(vmem_limit_bytes=40 << 20),
        cost_estimate=pl.CostEstimate(flops=gflops * 1_000_000_000, bytes_accessed=10 << 20, transcendentals=0),
    )(src, weights, *[p[0] for p in parts])


def gathered_weights(stack):
    count = stack.shape[0]
    wide = 2 * LANES - COEFFS
    by_source = jnp.pad(jnp.swapaxes(stack, 1, 2), ((0, 0), (0, wide), (0, wide)))
    packed = by_source.reshape(count, 2, LANES, 2 * LANES).transpose(0, 2, 1, 3).reshape(count * LANES, 4 * LANES)
    return lax.all_gather(packed, "lvl", axis=0, tiled=True)


def passed_along(block, axis, distance):
    devices = range(lax.axis_size(axis))
    route = [(i - distance, i) for i in devices if i - distance in devices]
    return lax.ppermute(block, axis, route)


def per_device(multipoles, fine_m2l, m2m, coarse_m2l, fine_source, ghost_index, ghost_count, owner, coarse_source):
    slab_count = lax.axis_size("slab")
    slab_here = lax.axis_index("slab")
    level_count = lax.axis_size("lvl")
    level_here = lax.axis_index("lvl")

    index_here = lax.dynamic_slice_in_dim(ghost_index, slab_here * GHOST, GHOST, 1)
    count_here = lax.dynamic_slice_in_dim(ghost_count, slab_here, 1, 1)
    inside = jnp.arange(GHOST, dtype=jnp.int32)[None, :] < count_here
    picks = jnp.where(inside, index_here, LEAVES).reshape(2 * GHOST // LANES, LANES)

    rows, sent = leaf_rows(multipoles, picks)
    upper = passed_along(sent[0], "slab", -1)
    lower = passed_along(sent[1], "slab", 1)

    owners = owner[:, 0]
    matches = (owners[:, None] == jnp.arange(slab_count, dtype=jnp.int32)[None, :]).astype(jnp.bfloat16)
    order = jnp.arange(PARENTS, dtype=jnp.int32)
    earlier = (order[None, :] < order[:, None]).astype(jnp.bfloat16)
    before = jnp.dot(earlier, matches, preferred_element_type=jnp.float32)
    rank = jnp.sum(before * matches.astype(jnp.float32), axis=1).astype(jnp.int32)
    capacity = SLOTS // slab_count
    place = (owners * capacity + rank).reshape(PARENTS // LANES, LANES)
    m2m_by_source = jnp.pad(jnp.swapaxes(m2m, 1, 2), ((0, 0), (0, 0), (0, 2 * LANES - COEFFS)))
    outgoing = placed_parents(multipoles, m2m_by_source, place)
    received = lax.all_to_all(
        outgoing.reshape(slab_count, capacity, 2, LANES), "slab", split_axis=0, concat_axis=0, tiled=True
    ).reshape(SLOTS, 2, LANES)

    fine_weights = gathered_weights(fine_m2l)
    coarse_weights = gathered_weights(coarse_m2l)

    quarter = LEAVES // level_count
    fine_targets = lax.dynamic_slice_in_dim(fine_source, level_here * quarter, quarter, 1)
    fine_local = translate(
        "fine",
        fine_targets,
        fine_weights,
        [
            (rows, 0, 0, LEAVES),
            (lower, LEAVES, 0, GHOST),
            (upper, LEAVES + GHOST, 0, GHOST),
            (rows, LEAVES + 2 * GHOST, LEAVES, TAIL),
        ],
        LEAVES + 2 * GHOST + TAIL,
        20,
    )
    coarse_quarter = SLOTS // level_count
    coarse_targets = lax.dynamic_slice_in_dim(coarse_source, level_here * coarse_quarter, coarse_quarter, 1)
    coarse_local = translate(
        "coarse",
        coarse_targets,
        coarse_weights,
        [(received, 0, 0, SLOTS), (rows, SLOTS, LEAVES, TAIL)],
        SLOTS + TAIL,
        6,
    )
    return (fine_local, coarse_local)


def solution(mesh):
    placed = (
        P(None, "slab"),
        P("lvl", None, None),
        P(),
        P("lvl", None, None),
        P(None, "slab"),
        P(),
        P(),
        P("slab", None),
        P(None, "slab"),
    )
    return jax.shard_map(
        per_device,
        mesh=mesh,
        in_specs=placed,
        out_specs=(P(None, ("slab", "lvl")), P(None, ("slab", "lvl"))),
        check_vma=False,
    )
```

time: 358 us -> 127 us (0.35)
  local copies, waits for them, and re-layouts: 232 us -> 22.4 us
  Pallas kernels: 0 us -> 62.8 us
  other arithmetic: 49 us -> 0.81 us
  matrix products: 20 us -> 0.59 us
  waiting for transfers between devices: 21.2 us -> 6.6 us
    gather x6 -> x0, local copies, waits for them, and re-layouts: 207 us -> none  [the longest x4 189 us: stack_products(): jnp.take(buffer_rows, flat_ids, axis=0)]
    pallas_call x0 -> x4, Pallas kernels: none -> 62.8 us  [the longest x2 41.7 us: translate(): pl.pallas_call(body, name=name, in_specs=[ANY, VMEM] + [ANY] * n, out_spe...]
    concatenate x1 -> x0, other arithmetic: 24.6 us -> none  [per_device(): buffer_rows = jnp.concatenate([own_rows, lower, upper, empty_row], axis=0)]
    dot_general x3 -> x1, matrix products: 20 us -> 0.59 us  [per_device(): before = jnp.dot(earlier, matches, preferred_element_type=jnp.float32)]
    all_to_all x1, waiting for transfers between devices: 19.8 us -> 1.04 us  [per_device(): lax.all_to_all(outgoing.reshape(slab_count, capacity, 2, LANES), 'slab',...]
    another operation x3 -> x0, other arithmetic: 18.2 us -> none
    ppermute x2 -> x0, local copies, waits for them, and re-layouts: 12.4 us -> none  [passed_along(): return lax.ppermute(block, axis, route)]
    unnamed x11 -> x28, local copies, waits for them, and re-layouts: 6.19 us -> 15.9 us
  transfers between devices with their start and end apart: 5 -> 5, of which waited for: 1 -> 2; matrix products, arithmetic and copies ran while one was open for 82% -> 6% of each run, Pallas kernels for 0% -> 24%
where the time goes in v1:
time: 127 us; the launch traced here: 126 us
  Pallas kernels  62.8 us (49%)
  local copies, waits for them, and re-layouts  22.4 us (18%)
  starting transfers between devices  18.5 us (15%)
  between operations  14.4 us (11%)
  waiting for transfers between devices  6.6 us (5%)
    pallas_call x2, Pallas kernels, translate(): pl.pallas_call(body, name=name, in_specs=[ANY, VMEM] + [ANY] * n, out_spe...  41.7 us
    unnamed x28, local copies, waits for them, and re-layouts  15.9 us
    pallas_call x1, Pallas kernels, leaf_rows(): pl.pallas_call(rows_body, name='leaf_rows', in_specs=[SMEM, VMEM], out_sp...  13 us
    all_to_all x1, starting transfers between devices, per_device(): lax.all_to_all(outgoing.reshape(slab_count, capacity, 2, LANES), 'slab',...  13 us
    pallas_call x1, Pallas kernels, placed_parents(): pl.pallas_call(parents_body, name='placed_parents', in_specs=[SMEM, VMEM,...  8.01 us
    all_gather x2, waiting for transfers between devices, gathered_weights(): return lax.all_gather(packed, 'lvl', axis=0, tiled=True)  5.52 us
    ppermute x2, starting transfers between devices, passed_along(): return lax.ppermute(block, axis, route)  5.45 us
  transfers between devices with their start and end apart: 5, of which 2 were waited for; matrix products, arithmetic and copies ran while one was open for 6% of the time, Pallas kernels for 24%

profile of v1, /device:TPU:1, one launch (start us, length us, event | category | flops | bytes accessed | tf_op | source)
XLA Modules:
  0.0 126.1 jit_solution(9806209410843472645)
XLA Ops:
  7.2 0.0 copy-start
  7.2 0.0 all-gather.5.cloned.1.call-start
  7.2 0.0 copy-start.9
  7.2 1.2 pad.12
  8.4 0.1 reshape.50
  8.5 0.7 copy.17
  9.2 0.9 copy.21
  10.1 0.0 all-gather.5.cloned.1.call-update
  10.1 0.0 all-gather.3.cloned.1.call-start
  10.2 0.0 copy-done.9
  10.2 0.0 copy-start.8
  10.2 0.1 pad.11
  10.3 0.1 reshape.45
  10.4 0.7 copy.15
  11.1 0.9 copy.20
  12.0 0.0 all-gather.3.cloned.1.call-update
  12.0 0.0 copy-done.8
  12.0 0.5 copy.18
  12.5 0.1 pad.13.w
  12.7 0.0 copy-done.10
  12.7 0.6 fusion.2
  13.3 0.0 copy-start.1
  13.3 2.0 %copy-done.1 = bf16[216,8192]{1,0:T(8,128)(2,1)S(1)} copy-done((bf16[216,8192]{1,0:T(8,128)(2,1)S(1)}, bf16[216,8192]{1,0:T(8,128)(2,1)}, u32[]{:S(2)}) %copy-start.1) | copy-done | bytes 3538968
  15.3 8.0 %placed_parents.1 = bf16[2048,2,128]{2,1,0:T(2,128)(2,1)} custom-call(s32[8,128]{1,0:T(8,128)S(1)} %bitcast_add_fusion.place, bf16[216,8192]{1,0:T(8,128)(2,1)S(1)} %copy-done.1, bf16[8,216,256]{2,1,0:T(8,128)(2,1)S(1)} %pad.13.w), custom_call_target="tpu_custom_call" | custom-call | flops 4000000000 | bytes 6291456 | tf_op jit(solution)/shard_map/placed_parents/pallas_call | solution.py:111
  23.4 0.0 copy-start.11
  23.4 13.0 %all-to-all-start = ((bf16[64,32,2,128]{3,2,1,0:T(2,128)(2,1)}), bf16[64,32,2,128]{3,2,1,0:T(2,128)(2,1)S(1)}, u32[]{:S(2)}, u32[]{:S(2)}) async-start(bf16[64,32,2,128]{3,2,1,0:T(2,128)(2,1)} %bitcast.12), calls=%async_computation | async-start | bytes 2097152 | tf_op jit(solution)/shard_map/all_to_all | solution.py:256
  36.4 0.0 copy-done.11
  36.4 0.2 dynamic-slice_reduce_fusion
  36.6 0.8 compare_select_fusion
  37.4 0.0 copy-start.2
  37.4 2.0 %copy-done.2 = bf16[216,8192]{1,0:T(8,128)(2,1)S(1)} copy-done((bf16[216,8192]{1,0:T(8,128)(2,1)S(1)}, bf16[216,8192]{1,0:T(8,128)(2,1)}, u32[]{:S(2)}) %copy-start.2) | copy-done | bytes 3538968
  39.4 13.0 %leaf_rows.1 = (bf16[8208,2,128]{2,1,0:T(2,128)(2,1)S(1)}, bf16[2,2048,2,128]{3,2,1,0:T(2,128)(2,1)S(1)}) custom-call(s32[32,128]{1,0:T(8,128)S(1)} %reshape.47.picks, bf16[216,8192]{1,0:T(8,128)(2,1)S(1)} %copy-done.2), custom_call_target="tpu_custom_call" | custom-call | flops 6000000000 | bytes 10485760 | tf_op jit(solution)/shard_map/leaf_rows/pallas_call | solution.py:61
  52.5 0.0 copy-start.5
  52.5 1.9 %copy-done.5 = bf16[8208,2,128]{2,1,0:T(2,128)(2,1)} copy-done((bf16[8208,2,128]{2,1,0:T(2,128)(2,1)}, bf16[8208,2,128]{2,1,0:T(2,128)(2,1)S(1)}, u32[]{:S(2)}) %copy-start.5) | copy-done | bytes 4202520
  54.4 2.4 %slice_bitcast_fusion = (bf16[2048,2,128]{2,1,0:T(2,128)(2,1)}, bf16[2048,2,128]{2,1,0:T(2,128)(2,1)}) fusion(bf16[2,2048,2,128]{3,2,1,0:T(2,128)(2,1)S(1)} %get-tuple-element.5), kind=kLoop, calls=%fused_computation.4 | loop fusion | bytes 4194304 | tf_op jit(solution)/shard_map/squeeze | solution.py:243
  56.9 3.5 %collective-permute-start = (bf16[2048,2,128]{2,1,0:T(2,128)(2,1)}, bf16[2048,2,128]{2,1,0:T(2,128)(2,1)S(1)}, u32[]{:S(2)}, u32[]{:S(2)}) collective-permute-start(bf16[2048,2,128]{2,1,0:T(2,128)(2,1)} %get-tuple-element.7), channel_id=1, source_target_pairs={{0,4},{4,8},{8,12},{12,16},{16,20},{20,24},{24,28},{28,32},{32,36}... | collective-permute-start | bytes 3145736 | tf_op jit(solution)/shard_map/ppermute | solution.py:228
  60.4 1.9 %collective-permute-start.1 = (bf16[2048,2,128]{2,1,0:T(2,128)(2,1)}, bf16[2048,2,128]{2,1,0:T(2,128)(2,1)}, u32[]{:S(2)}, u32[]{:S(2)}) collective-permute-start(bf16[2048,2,128]{2,1,0:T(2,128)(2,1)} %get-tuple-element.6), channel_id=1, source_target_pairs={{4,0},{8,4},{12,8},{16,12},{20,16},{24,20},{28,24},{32,28},{36,32}... | collective-permute-start | bytes 3145736 | tf_op jit(solution)/shard_map/ppermute | solution.py:228
  62.5 0.8 constant_dynamic-slice_fusion
  63.3 1.0 all-to-all-done
  64.4 1.6 %copy-done.3 = bf16[2048,512]{1,0:T(8,128)(2,1)S(1)} copy-done((bf16[2048,512]{1,0:T(8,128)(2,1)S(1)}, bf16[2048,512]{1,0:T(8,128)(2,1)}, u32[]{:S(2)}) %copy-start.3) | copy-done | bytes 2097176
  66.0 2.2 %copy-done.6 = bf16[8208,2,128]{2,1,0:T(2,128)(2,1)S(1)} copy-done((bf16[8208,2,128]{2,1,0:T(2,128)(2,1)S(1)}, bf16[8208,2,128]{2,1,0:T(2,128)(2,1)}, u32[]{:S(2)}) %copy-start.6) | copy-done | bytes 4202520
  68.1 9.1 %coarse.1 = f32[216,512]{1,0:T(8,128)} custom-call(s32[2,32,128]{2,1,0:T(8,128)S(1)} %reshape.49.src_ref, bf16[2048,512]{1,0:T(8,128)(2,1)S(1)} %copy-done.3, bf16[2048,2,128]{2,1,0:T(2,128)(2,1)S(1)} %bitcast.30, bf16[8208,2,128]{2,1,0:T(2,128)(2,1)S(1)} %copy-done.6), custom_call_target="tpu_custom_call" | custom-call | flops 6000000000 | bytes 10485760 | tf_op jit(solution)/shard_map/coarse/pallas_call | solution.py:194
  77.3 0.0 collective-permute-done.refs_1_
  77.3 0.0 collective-permute-done.1.refs_2_
  77.3 5.5 %all-gather.3.cloned.1.call-done.w = bf16[2048,512]{1,0:T(8,128)(2,1)} async-done(((bf16[512,512]{1,0:T(8,128)(2,1)}), bf16[2048,512]{1,0:T(8,128)(2,1)}) %all-gather.3.cloned.1.call-update) | async-done | bytes 2097168 | tf_op jit(solution)/shard_map/all_gather | solution.py:222
  82.8 1.6 %copy-done.4 = bf16[2048,512]{1,0:T(8,128)(2,1)S(1)} copy-done((bf16[2048,512]{1,0:T(8,128)(2,1)S(1)}, bf16[2048,512]{1,0:T(8,128)(2,1)}, u32[]{:S(2)}) %copy-start.4) | copy-done | bytes 2097176
  84.4 2.2 %copy-done.7 = bf16[8208,2,128]{2,1,0:T(2,128)(2,1)S(1)} copy-done((bf16[8208,2,128]{2,1,0:T(2,128)(2,1)S(1)}, bf16[8208,2,128]{2,1,0:T(2,128)(2,1)}, u32[]{:S(2)}) %copy-start.7) | copy-done | bytes 4202520
  86.6 32.6 %fine.1 = f32[216,2048]{1,0:T(8,128)} custom-call(s32[8,32,128]{2,1,0:T(8,128)S(1)} %reshape.44.src_ref, bf16[2048,512]{1,0:T(8,128)(2,1)S(1)} %copy-done.4, bf16[8208,2,128]{2,1,0:T(2,128)(2,1)S(1)} %copy-done.7, bf16[2048,2,128]{2,1,0:T(2,128)(2,1)S(1)} %collective-permute-done.refs_1_, bf16[2048,2,128]{2,1,0:T(2,128)(2,1)} %collective-permute-done.1.refs_2_, ...), custom_call_target="tpu_custom_call" | custom-call | flops 20000000000 | bytes 10485760 | tf_op jit(solution)/shard_map/fine/pallas_call | solution.py:194
  (17 shorter events, 0.2 us)
Async XLA Ops:
  7.2 55.2 %copy-start = (s32[16,8192]{1,0:T(8,128)S(1)}, s32[16,8192]{1,0:T(8,128)}, u32[]{:S(2)}) copy-start(s32[16,8192]{1,0:T(8,128)} %param.13) | copy-start | bytes 1572868
  7.2 57.2 %all-gather.5.cloned.1.call-start = ((), (), s32[]{:S(2)}) async-start(), calls=%async_computation.2 | async-start | bytes 2621440 | tf_op jit(solution)/shard_map/all_gather | solution.py:222
  7.2 3.0 %copy-start.9 = (bf16[4,216,216]{2,1,0:T(8,128)(2,1)S(1)}, bf16[4,216,216]{2,1,0:T(8,128)(2,1)}, u32[]{:S(2)}) copy-start(bf16[4,216,216]{2,1,0:T(8,128)(2,1)} %param.10) | copy-start | bytes 1119748
  10.1 72.7 %all-gather.3.cloned.1.call-start = ((), (), s32[]{:S(2)}) async-start(), calls=%async_computation.1 | async-start | bytes 2621440 | tf_op jit(solution)/shard_map/all_gather | solution.py:222
  10.2 1.8 %copy-start.8 = (bf16[8,216,216]{2,1,0:T(8,128)(2,1)S(1)}, bf16[8,216,216]{2,1,0:T(8,128)(2,1)}, u32[]{:S(2)}) copy-start(bf16[8,216,216]{2,1,0:T(8,128)(2,1)} %param.11) | copy-start | bytes 2239492
  12.0 0.7 copy-start.10
  13.3 2.0 %copy-start.1 = (bf16[216,8192]{1,0:T(8,128)(2,1)S(1)}, bf16[216,8192]{1,0:T(8,128)(2,1)}, u32[]{:S(2)}) copy-start(bf16[216,8192]{1,0:T(8,128)(2,1)} %x.9) | copy-start | bytes 10616836
  23.4 13.0 %copy-start.11 = (s32[2,64]{1,0:T(2,128)S(1)}, s32[2,64]{1,0:T(2,128)}, u32[]{:S(2)}) copy-start(s32[2,64]{1,0:T(2,128)} %param.15) | copy-start | bytes 1540
  23.4 41.0 %all-to-all-start = ((bf16[64,32,2,128]{3,2,1,0:T(2,128)(2,1)}), bf16[64,32,2,128]{3,2,1,0:T(2,128)(2,1)S(1)}, u32[]{:S(2)}, u32[]{:S(2)}) async-start(bf16[64,32,2,128]{3,2,1,0:T(2,128)(2,1)} %bitcast.12), calls=%async_computation | async-start | bytes 2097152 | tf_op jit(solution)/shard_map/all_to_all | solution.py:256
  37.4 2.0 %copy-start.2 = (bf16[216,8192]{1,0:T(8,128)(2,1)S(1)}, bf16[216,8192]{1,0:T(8,128)(2,1)}, u32[]{:S(2)}) copy-start(bf16[216,8192]{1,0:T(8,128)(2,1)} %x.9) | copy-start | bytes 10616836
  52.5 2.0 %copy-start.5 = (bf16[8208,2,128]{2,1,0:T(2,128)(2,1)}, bf16[8208,2,128]{2,1,0:T(2,128)(2,1)S(1)}, u32[]{:S(2)}) copy-start(bf16[8208,2,128]{2,1,0:T(2,128)(2,1)S(1)} %get-tuple-element.4.refs_0_.refs_3_.refs_1_) | copy-start | bytes 12607492
  56.9 20.4 %collective-permute-start = (bf16[2048,2,128]{2,1,0:T(2,128)(2,1)}, bf16[2048,2,128]{2,1,0:T(2,128)(2,1)S(1)}, u32[]{:S(2)}, u32[]{:S(2)}) collective-permute-start(bf16[2048,2,128]{2,1,0:T(2,128)(2,1)} %get-tuple-element.7), channel_id=1, source_target_pairs={{0,4},{4,8},{8,12},{12,16},{16,20},{20,24},{24,28},{28,32},{32,36}... | collective-permute-start | bytes 3145736 | tf_op jit(solution)/shard_map/ppermute | solution.py:228
  60.4 16.9 %collective-permute-start.1 = (bf16[2048,2,128]{2,1,0:T(2,128)(2,1)}, bf16[2048,2,128]{2,1,0:T(2,128)(2,1)}, u32[]{:S(2)}, u32[]{:S(2)}) collective-permute-start(bf16[2048,2,128]{2,1,0:T(2,128)(2,1)} %get-tuple-element.6), channel_id=1, source_target_pairs={{4,0},{8,4},{12,8},{16,12},{20,16},{24,20},{28,24},{32,28},{36,32}... | collective-permute-start | bytes 3145736 | tf_op jit(solution)/shard_map/ppermute | solution.py:228
  64.4 1.6 %copy-start.3 = (bf16[2048,512]{1,0:T(8,128)(2,1)S(1)}, bf16[2048,512]{1,0:T(8,128)(2,1)}, u32[]{:S(2)}) copy-start(bf16[2048,512]{1,0:T(8,128)(2,1)} %all-gather.5.cloned.1.call-done.w) | copy-start | bytes 6291460
  66.0 2.2 %copy-start.6 = (bf16[8208,2,128]{2,1,0:T(2,128)(2,1)S(1)}, bf16[8208,2,128]{2,1,0:T(2,128)(2,1)}, u32[]{:S(2)}) copy-start(bf16[8208,2,128]{2,1,0:T(2,128)(2,1)} %copy-done.5) | copy-start | bytes 12607492
  82.8 1.6 %copy-start.4 = (bf16[2048,512]{1,0:T(8,128)(2,1)S(1)}, bf16[2048,512]{1,0:T(8,128)(2,1)}, u32[]{:S(2)}) copy-start(bf16[2048,512]{1,0:T(8,128)(2,1)} %all-gather.3.cloned.1.call-done.w) | copy-start | bytes 6291460
  84.4 2.2 %copy-start.7 = (bf16[8208,2,128]{2,1,0:T(2,128)(2,1)S(1)}, bf16[8208,2,128]{2,1,0:T(2,128)(2,1)}, u32[]{:S(2)}) copy-start(bf16[8208,2,128]{2,1,0:T(2,128)(2,1)} %copy-done.5) | copy-start | bytes 12607492
Sparse Core Ops, SparseCore 0:
  10.2 37.2 all-gather.4
  49.3 33.4 all-gather.2

commit v2 on v1

v2 whole, which is shorter than its diff:
```python
import jax
import jax.numpy as jnp
from jax import lax
from jax.experimental import pallas as pl
from jax.experimental.pallas import tpu as pltpu
from jax.sharding import PartitionSpec as P

COEFFS = 216
LANES = 128
OPS = 16
TILE = 512
LEAVES = 8192
GHOST = 2048
PARENTS = 1024
SLOTS = 2048
TAIL = 16
BLOCK = 256
GROUP = 2048
CHUNKS = 8

ANY = pl.BlockSpec(memory_space=pl.ANY)
VMEM = pl.BlockSpec(memory_space=pltpu.VMEM)
SMEM = pl.BlockSpec(memory_space=pltpu.SMEM)


def contract_lanes(a, b):
    return lax.dot_general(a, b, (((1,), (1,)), ((), ())), preferred_element_type=jnp.float32)


def rows_body(picks, x_hbm, rows_hbm, down, up, x, spread, stage, rows, sent, xsem, osem):
    chunk = LEAVES // CHUNKS
    loads = []
    for k in range(CHUNKS):
        part = (slice(None), pl.ds(k * chunk, chunk))
        loads.append(pltpu.make_async_copy(x_hbm.at[part], x.at[part], xsem.at[k]))
        loads[k].start()
    r = lax.broadcasted_iota(jnp.int32, (2 * LANES, 2 * LANES), 0)
    c = lax.broadcasted_iota(jnp.int32, (2 * LANES, 2 * LANES), 1)
    spread[...] = jnp.where(r == 2 * (c % LANES) + c // LANES, 1.0, 0.0).astype(jnp.bfloat16)
    rows[pl.ds(2 * LEAVES, 2 * TAIL)] = jnp.zeros((2 * TAIL, LANES), jnp.float32)
    empty = jnp.zeros((2 * LANES - COEFFS, LANES), jnp.bfloat16)

    keeps = []
    for k in range(CHUNKS):
        loads[k].wait()
        for b in range(k * chunk // BLOCK, (k + 1) * chunk // BLOCK):
            halves = []
            for start in (b * BLOCK, b * BLOCK + LANES):
                cols = slice(start, start + LANES)
                high = jnp.concatenate([x[LANES:COEFFS, cols], empty], axis=0)
                halves.append(jnp.concatenate([x[0:LANES, cols], high], axis=1))
            both = contract_lanes(spread[...], jnp.concatenate(halves, axis=0))
            for h in range(2):
                here = pl.ds((2 * b + h) * BLOCK, BLOCK)
                rows[here] = both[:, h * LANES : (h + 1) * LANES]
                stage[here] = both[:, h * LANES : (h + 1) * LANES].astype(jnp.bfloat16)
        here = pl.ds(k * 2 * chunk, 2 * chunk)
        keeps.append(pltpu.make_async_copy(stage.at[here], rows_hbm.at[here], osem.at[k]))
        keeps[k].start()

    for d, out in enumerate((down, up)):
        for g in range(GHOST):
            f = d * GHOST + g
            sent[g] = rows[pl.ds(picks[f // LANES, f % LANES], 2), :]
        out[...] = sent.reshape(2 * GHOST, LANES)[...].astype(jnp.bfloat16)
    for keep in keeps:
        keep.wait()


def leaf_rows(multipoles, picks):
    ghosts = jax.ShapeDtypeStruct((2 * GHOST, LANES), jnp.bfloat16)
    return pl.pallas_call(
        rows_body,
        name="leaf_rows",
        in_specs=[SMEM, ANY],
        out_specs=[ANY, VMEM, VMEM],
        out_shape=[jax.ShapeDtypeStruct((2 * LEAVES, LANES), jnp.bfloat16), ghosts, ghosts],
        scratch_shapes=[
            pltpu.VMEM((COEFFS, LEAVES), jnp.bfloat16),
            pltpu.VMEM((2 * LANES, 2 * LANES), jnp.bfloat16),
            pltpu.VMEM((2 * LEAVES, LANES), jnp.bfloat16),
            pltpu.VMEM((2 * (LEAVES + TAIL), LANES), jnp.float32),
            pltpu.VMEM((GHOST, 2, LANES), jnp.float32),
            pltpu.SemaphoreType.DMA((CHUNKS,)),
            pltpu.SemaphoreType.DMA((CHUNKS,)),
        ],
        compiler_params=pltpu.CompilerParams(vmem_limit_bytes=60 << 20),
        cost_estimate=pl.CostEstimate(flops=6_000_000_000, bytes_accessed=10 << 20, transcendentals=0),
    )(picks, multipoles)


def parents_body(place, x_hbm, w_hbm, out, x, w, children, rows, placed, xsem, wsem):
    groups = LEAVES // GROUP
    loads = []
    for k in range(groups):
        part = (slice(None), pl.ds(k * GROUP, GROUP))
        loads.append(pltpu.make_async_copy(x_hbm.at[part], x.at[part], xsem.at[k]))
        loads[k].start()
    weights = pltpu.make_async_copy(w_hbm, w, wsem)
    weights.start()
    placed[...] = jnp.zeros_like(placed)
    per_block = BLOCK // 8
    r = lax.broadcasted_iota(jnp.int32, (BLOCK, BLOCK), 0)
    c = lax.broadcasted_iota(jnp.int32, (BLOCK, BLOCK), 1)
    octant_major = jnp.where(c == (r % per_block) * 8 + r // per_block, 1.0, 0.0).astype(jnp.bfloat16)
    per_group = GROUP // 8
    empty = jnp.zeros((per_group, 2 * LANES - COEFFS), jnp.float32)

    for s in range(groups):
        loads[s].wait()
        for b in range(GROUP // BLOCK):
            start = s * GROUP + b * BLOCK
            sorted_rows = contract_lanes(octant_major, x[:, start : start + BLOCK]).astype(jnp.bfloat16)
            for o in range(8):
                children[o, b * per_block : (b + 1) * per_block] = sorted_rows[o * per_block : (o + 1) * per_block]
        if s == 0:
            weights.wait()
        total = contract_lanes(children[0], w[0])
        for o in range(1, 8):
            total += contract_lanes(children[o], w[o])
        first = s * 2 * per_group
        rows[pl.ds(first, per_group, 2), :] = total[:, :LANES]
        rows[pl.ds(first + 1, per_group, 2), :] = jnp.concatenate([total[:, LANES:], empty], axis=1)

    box = rows.reshape(PARENTS, 2, LANES)
    for p in range(PARENTS):
        placed[pl.ds(place[p // LANES, p % LANES], 2), :] = box[p]
    out[...] = placed[...].astype(jnp.bfloat16)


def placed_parents(multipoles, weights, place):
    return pl.pallas_call(
        parents_body,
        name="placed_parents",
        in_specs=[SMEM, ANY, ANY],
        out_specs=VMEM,
        out_shape=jax.ShapeDtypeStruct((2 * SLOTS, LANES), jnp.bfloat16),
        scratch_shapes=[
            pltpu.VMEM((COEFFS, LEAVES), jnp.bfloat16),
            pltpu.VMEM((8, COEFFS, COEFFS), jnp.bfloat16),
            pltpu.VMEM((8, GROUP // 8, COEFFS), jnp.bfloat16),
            pltpu.VMEM((2 * PARENTS, LANES), jnp.float32),
            pltpu.VMEM((2 * SLOTS, LANES), jnp.float32),
            pltpu.SemaphoreType.DMA((LEAVES // GROUP,)),
            pltpu.SemaphoreType.DMA(()),
        ],
        compiler_params=pltpu.CompilerParams(vmem_limit_bytes=60 << 20),
        cost_estimate=pl.CostEstimate(flops=4_000_000_000, bytes_accessed=6 << 20, transcendentals=0),
    )(place, multipoles, weights)


def translate(name, sources, which_core, weights, swapped, parts, gflops):
    targets = sources.shape[1]
    tiles = targets // TILE
    n = len(parts)
    width = OPS * TILE // LANES
    src = sources.reshape(OPS, tiles, TILE).swapaxes(0, 1).reshape(tiles * width, LANES)
    sizes = [p.shape[0] for p in parts]
    starts = [sum(sizes[:k]) for k in range(n)]
    slots = sum(sizes)
    piece = 2048
    pieces = [(k, at) for k in range(n) for at in range(0, sizes[k], piece)]

    def body(core, src_ref, *refs):
        here, mine, other = refs[0], refs[1:4], refs[4:7]
        refs = refs[7:]
        part_refs = refs[:n]
        out = refs[n]
        stage, buf, z, raw, w, psem, wsem = refs[n + 1 :]
        copies = []
        for j, (k, at) in enumerate(pieces):
            into = stage.at[pl.ds(starts[k] + at, piece)]
            copies.append(pltpu.make_async_copy(part_refs[k].at[pl.ds(at, piece)], into, psem.at[j]))

        pltpu.make_async_copy(here, raw.at[pl.ds(0, 4)], wsem.at[0]).start()
        for q in range(3):
            into = raw.at[pl.ds(4 * q + 4, 4)]

            @pl.when(core[0] != swapped)
            def _():
                pltpu.make_async_copy(mine[q], into, wsem.at[q + 1]).start()

            @pl.when(core[0] == swapped)
            def _():
                pltpu.make_async_copy(other[q], into, wsem.at[q + 1]).start()

        for copy in copies:
            copy.start()
        for q in range(4):
            pltpu.make_async_copy(here, raw.at[pl.ds(4 * q, 4)], wsem.at[q]).wait()
        r = lax.broadcasted_iota(jnp.int32, (2 * LANES, COEFFS), 0)
        c = lax.broadcasted_iota(jnp.int32, (2 * LANES, COEFFS), 1)
        unit = jnp.where(r == c, 1.0, 0.0).astype(jnp.bfloat16)
        for o in range(OPS):
            w[o * 2 * LANES : (o + 1) * 2 * LANES] = contract_lanes(unit, raw[o]).astype(jnp.bfloat16)

        buf[pl.ds(slots, 2 * TAIL)] = jnp.zeros((2 * TAIL, LANES), jnp.float32)
        for copy, (k, at) in zip(copies, pieces):
            copy.wait()
            now = pl.ds(starts[k] + at, piece)
            buf[now] = stage[now].astype(jnp.float32)

        @pl.loop(0, tiles)
        def _(tile):
            for o in range(OPS):
                for u in range(TILE):
                    f = o * TILE + u
                    slot = src_ref.at[:, pl.ds(f % LANES, 1)][tile * width + f // LANES, 0]
                    z[o, u] = buf[pl.ds(slot, 2), :]
            halves = []
            for o in range(OPS):
                box = z.at[o].reshape(2 * TILE, LANES)
                for h in range(2):
                    halves.append(box[pl.ds(h, TILE, 2), :].astype(jnp.bfloat16))
            total = jnp.dot(jnp.concatenate(halves, axis=1), w[...], preferred_element_type=jnp.float32)
            columns = pl.ds(pl.multiple_of(tile * TILE, TILE), TILE)
            out[:, columns] = total.T

    return pl.pallas_call(
        body,
        name=name,
        in_specs=[SMEM, SMEM] + [ANY] * (7 + n),
        out_specs=VMEM,
        out_shape=jax.ShapeDtypeStruct((COEFFS, targets), jnp.float32),
        scratch_shapes=[
            pltpu.VMEM((slots, LANES), jnp.bfloat16),
            pltpu.VMEM((slots + 2 * TAIL, LANES), jnp.float32),
            pltpu.VMEM((OPS, TILE, 2, LANES), jnp.float32),
            pltpu.VMEM((OPS, COEFFS, COEFFS), jnp.bfloat16),
            pltpu.VMEM((OPS * 2 * LANES, COEFFS), jnp.bfloat16),
            pltpu.SemaphoreType.DMA((len(pieces),)),
            pltpu.SemaphoreType.DMA((4,)),
        ],
        compiler_params=pltpu.CompilerParams(vmem_limit_bytes=60 << 20),
        cost_estimate=pl.CostEstimate(flops=gflops * 1_000_000_000, bytes_accessed=10 << 20, transcendentals=0),
    )(which_core, src, *weights, *parts)


def passed_along(block, axis, distance):
    devices = range(lax.axis_size(axis))
    route = [(i - distance, i) for i in devices if i - distance in devices]
    return lax.ppermute(block, axis, route)


def turned(block, distance):
    size = lax.axis_size("lvl")
    return lax.ppermute(block, "lvl", [((i + distance) % size, i) for i in range(size)])


def swapped_cores(block):
    return lax.ppermute(block, "slab", [(i ^ 1, i) for i in range(lax.axis_size("slab"))])


def sources_here(sources, level_here, level_count):
    quarter = sources.shape[1] // level_count
    here = 2 * lax.dynamic_slice_in_dim(sources, level_here * quarter, quarter, 1)
    return lax.dynamic_slice_in_dim(jnp.concatenate([here, here], axis=0), level_here * (OPS // level_count), OPS, 0)


def per_device(multipoles, fine_m2l, m2m, coarse_m2l, fine_source, ghost_index, ghost_count, owner, coarse_source):
    slab_count = lax.axis_size("slab")
    slab_here = lax.axis_index("slab")
    level_count = lax.axis_size("lvl")
    level_here = lax.axis_index("lvl")

    core = slab_here % 2
    fetched = jnp.where(core == 0, fine_m2l, coarse_m2l)
    mine = [turned(fetched, d) for d in (1, 2, 3)]
    other = [swapped_cores(m) for m in mine]
    core_flag = core.astype(jnp.int32).reshape(1)

    index_here = lax.dynamic_slice_in_dim(ghost_index, slab_here * GHOST, GHOST, 1)
    count_here = lax.dynamic_slice_in_dim(ghost_count, slab_here, 1, 1)
    inside = jnp.arange(GHOST, dtype=jnp.int32)[None, :] < count_here
    picks = jnp.where(inside, 2 * index_here, 2 * LEAVES).reshape(2 * GHOST // LANES, LANES)
    rows, down, up = leaf_rows(multipoles, picks)
    upper = passed_along(down, "slab", -1)
    lower = passed_along(up, "slab", 1)

    owners = owner[:, 0]
    matches = (owners[:, None] == jnp.arange(slab_count, dtype=jnp.int32)[None, :]).astype(jnp.bfloat16)
    order = jnp.arange(PARENTS, dtype=jnp.int32)
    earlier = (order[None, :] < order[:, None]).astype(jnp.bfloat16)
    before = jnp.dot(earlier, matches, preferred_element_type=jnp.float32)
    rank = jnp.sum(before * matches.astype(jnp.float32), axis=1).astype(jnp.int32)
    capacity = SLOTS // slab_count
    place = (2 * (owners * capacity + rank)).reshape(PARENTS // LANES, LANES)
    place, rows = lax.optimization_barrier((place, rows))
    outgoing = placed_parents(multipoles, m2m, place)
    received = lax.all_to_all(
        outgoing.reshape(slab_count, 2 * capacity, LANES), "slab", split_axis=0, concat_axis=0, tiled=True
    ).reshape(2 * SLOTS, LANES)

    fine_local = translate(
        "fine",
        sources_here(fine_source, level_here, level_count),
        core_flag,
        [fine_m2l, *mine, *other],
        1,
        [rows, lower, upper],
        20,
    )
    coarse_local = translate(
        "coarse",
        sources_here(coarse_source, level_here, level_count),
        core_flag,
        [coarse_m2l, *mine, *other],
        0,
        [received],
        6,
    )
    return (fine_local, coarse_local)


def solution(mesh):
    placed = (
        P(None, "slab"),
        P("lvl", None, None),
        P(),
        P("lvl", None, None),
        P(None, "slab"),
        P(),
        P(),
        P("slab", None),
        P(None, "slab"),
    )
    return jax.shard_map(
        per_device,
        mesh=mesh,
        in_specs=placed,
        out_specs=(P(None, ("slab", "lvl")), P(None, ("slab", "lvl"))),
        check_vma=False,
    )
```

time: 127 us -> 99.4 us (0.78)
  local copies, waits for them, and re-layouts: 22.4 us -> 4.17 us
  between operations: 14.4 us -> 0.99 us
  starting transfers between devices: 18.5 us -> 25.3 us
  waiting for transfers between devices: 6.6 us -> 0.28 us
  other arithmetic: 0.81 us -> 4.21 us
    unnamed x28 -> x12, local copies, waits for them, and re-layouts: 15.9 us -> 1.96 us
    ppermute x0 -> x6, starting transfers between devices: none -> 5.73 us  [the longest x3 4.68 us: turned(): lax.ppermute(block, 'lvl', [((i + distance) % size, i) for i in range(siz...]
    all_gather x2 -> x0, waiting for transfers between devices: 5.52 us -> none  [gathered_weights(): return lax.all_gather(packed, 'lvl', axis=0, tiled=True)]
    squeeze x1 -> x0, local copies, waits for them, and re-layouts: 2.44 us -> none  [per_device(): upper = passed_along(sent[0], 'slab', -1)]
    mul x1 -> x4, other arithmetic: 0.01 us -> 2.29 us  [the longest x2 1.68 us: sources_here(): 2 * lax.dynamic_slice_in_dim(sources, level_here * quarter, quarter, 1)]
    pad x3 -> x0, local copies, waits for them, and re-layouts: 1.39 us -> none  [the longest x2 1.24 us: gathered_weights(): jnp.pad(jnp.swapaxes(stack, 1, 2), ((0, 0), (0, wide), (0, wide)))]
  transfers between devices with their start and end apart: 5 -> 9, of which waited for: 2 -> 2; matrix products, arithmetic and copies ran while one was open for 6% -> 6% of each run, Pallas kernels for 24% -> 53%
where the time goes in v2:
time: 99.4 us; the launch traced here: 98.7 us
  Pallas kernels  63.1 us (63%)
  starting transfers between devices  25.3 us (25%)
  other arithmetic  4.21 us (4%)
  local copies, waits for them, and re-layouts  4.17 us (4%)
    pallas_call x2, Pallas kernels, translate(): pl.pallas_call(body, name=name, in_specs=[SMEM, SMEM] + [ANY] * (7 + n),...  43.2 us
    all_to_all x1, starting transfers between devices, per_device(): lax.all_to_all(outgoing.reshape(slab_count, 2 * capacity, LANES), 'slab',...  13 us
    pallas_call x1, Pallas kernels, leaf_rows(): pl.pallas_call(rows_body, name='leaf_rows', in_specs=[SMEM, ANY], out_spe...  11.3 us
    pallas_call x1, Pallas kernels, placed_parents(): pl.pallas_call(parents_body, name='placed_parents', in_specs=[SMEM, ANY,...  8.71 us
    ppermute x2, starting transfers between devices, passed_along(): return lax.ppermute(block, axis, route)  6.6 us
    ppermute x3, starting transfers between devices, turned(): lax.ppermute(block, 'lvl', [((i + distance) % size, i) for i in range(siz...  4.68 us
  transfers between devices with their start and end apart: 9, of which 2 were waited for; matrix products, arithmetic and copies ran while one was open for 6% of the time, Pallas kernels for 53%

profile of v2, /device:TPU:1, one launch (start us, length us, event | category | flops | bytes accessed | tf_op | source)
XLA Modules:
  0.0 98.7 jit_solution(15998109255157262644)
XLA Ops:
  0.6 0.0 copy-start
  0.7 1.1 %broadcast_select_fusion = bf16[4,216,216]{2,1,0:T(8,128)(2,1)S(1)} fusion(bf16[4,216,216]{2,1,0:T(8,128)(2,1)} %refs_0_.2, bf16[4,216,216]{2,1,0:T(8,128)(2,1)} %refs_0_.3, pred[]{:T(512)S(6)} %eq.20), kind=kLoop, calls=%fused_computation.4 | loop fusion | flops 186624 | bytes 1119745 | tf_op jit(solution)/shard_map/jit(_where)/select_n | solution.py:267
  1.7 3.6 %collective-permute-start = (bf16[4,216,216]{2,1,0:T(8,128)(2,1)S(1)}, bf16[4,216,216]{2,1,0:T(8,128)(2,1)S(1)}, u32[]{:S(2)}, u32[]{:S(2)}) collective-permute-start(bf16[4,216,216]{2,1,0:T(8,128)(2,1)S(1)} %broadcast_select_fusion), channel_id=1, source_target_pairs={{1,0},{2,1},{3,2},{0,3},{5,4},{6,5},{7,6},{4,7},{9,8},{10,9},{11,1... | collective-permute-start | bytes 1119752 | tf_op jit(solution)/shard_map/ppermute | solution.py:247
  5.4 0.3 collective-permute-start.1
  5.7 0.7 collective-permute-start.2
  6.4 0.0 copy-done
  6.4 0.2 fusion.8
  6.6 0.8 compare_select_fusion
  7.4 0.6 reshape.31.picks
  8.0 0.0 copy-start.2
  8.0 11.3 %leaf_rows.1 = (bf16[16384,128]{1,0:T(8,128)(2,1)}, bf16[4096,128]{1,0:T(8,128)(2,1)}, bf16[4096,128]{1,0:T(8,128)(2,1)}) custom-call(s32[32,128]{1,0:T(8,128)} %reshape.31.picks, bf16[216,8192]{1,0:T(8,128)(2,1)} %x_hbm.3), custom_call_target="tpu_custom_call" | custom-call | flops 6000000000 | bytes 10485760 | tf_op jit(solution)/shard_map/leaf_rows/pallas_call | solution.py:72
  19.3 4.5 %collective-permute-start.6 = (bf16[4096,128]{1,0:T(8,128)(2,1)}, bf16[4096,128]{1,0:T(8,128)(2,1)S(1)}, u32[]{:S(2)}, u32[]{:S(2)}) collective-permute-start(bf16[4096,128]{1,0:T(8,128)(2,1)} %get-tuple-element.9), channel_id=1, source_target_pairs={{0,4},{4,8},{8,12},{12,16},{16,20},{20,24},{24,28},{28,32},{32,36}... | collective-permute-start | bytes 3145736 | tf_op jit(solution)/shard_map/ppermute | solution.py:242
  23.8 2.1 %collective-permute-start.7 = (bf16[4096,128]{1,0:T(8,128)(2,1)}, bf16[4096,128]{1,0:T(8,128)(2,1)}, u32[]{:S(2)}, u32[]{:S(2)}) collective-permute-start(bf16[4096,128]{1,0:T(8,128)(2,1)} %get-tuple-element.10), channel_id=1, source_target_pairs={{4,0},{8,4},{12,8},{16,12},{20,16},{24,20},{28,24},{32,28},{36,32}... | collective-permute-start | bytes 3145736 | tf_op jit(solution)/shard_map/ppermute | solution.py:242
  25.9 0.0 copy-done.2
  25.9 0.6 fusion.2
  26.5 0.6 fusion.7.place
  27.1 8.7 %placed_parents.1 = bf16[4096,128]{1,0:T(8,128)(2,1)} custom-call(s32[8,128]{1,0:T(8,128)} %fusion.7.place, bf16[216,8192]{1,0:T(8,128)(2,1)} %x_hbm.3, bf16[8,216,216]{2,1,0:T(8,128)(2,1)} %w_hbm.1), custom_call_target="tpu_custom_call" | custom-call | flops 4000000000 | bytes 6291456 | tf_op jit(solution)/shard_map/placed_parents/pallas_call | solution.py:132
  35.8 13.0 %all-to-all-start = ((bf16[64,64,128]{2,1,0:T(8,128)(2,1)}), bf16[64,64,128]{2,1,0:T(8,128)(2,1)S(1)}, u32[]{:S(2)}, u32[]{:S(2)}) async-start(bf16[64,64,128]{2,1,0:T(8,128)(2,1)} %bitcast.11), calls=%async_computation | async-start | bytes 2097152 | tf_op jit(solution)/shard_map/all_to_all | solution.py:290
  48.9 0.9 dynamic-slice_multiply_fusion
  49.8 0.0 collective-permute-done.refs_1_
  49.8 0.0 copy-start.4
  49.8 0.5 collective-permute-start.3
  50.3 0.0 collective-permute-done.1.refs_2_
  50.3 0.0 copy-start.5
  50.3 0.1 collective-permute-start.4
  50.5 0.0 collective-permute-done.2.refs_3_
  50.5 0.4 collective-permute-start.5
  50.9 0.1 reshape.29
  51.1 0.7 reshape.30.src_ref
  51.7 0.8 dynamic-slice_multiply_fusion.1
  52.5 0.6 reshape_transpose_reshape.3.src_ref
  53.1 0.0 collective-permute-done.3.refs_4_
  53.1 0.1 collective-permute-done.4.refs_5_
  53.2 0.2 collective-permute-done.5.refs_6_
  53.4 0.0 collective-permute-done.6.refs_8_
  53.4 0.0 copy-start.3
  53.4 0.0 collective-permute-done.7.refs_9_
  53.4 0.0 copy-done.4
  53.4 0.0 copy-done.5
  53.4 1.0 copy-done.3
  54.4 32.8 %fine.1 = f32[216,2048]{1,0:T(8,128)} custom-call(s32[1]{0:T(128)} %bitcast.core, s32[256,128]{1,0:T(8,128)} %reshape.30.src_ref, bf16[4,216,216]{2,1,0:T(8,128)(2,1)} %refs_0_.2, bf16[4,216,216]{2,1,0:T(8,128)(2,1)} %copy-done.4, bf16[4,216,216]{2,1,0:T(8,128)(2,1)} %copy-done.5, bf16[4,216,216]{2,1,0:T(8,128)(2,1)} %collective-permute-done.2.refs_3_, ...), custom_call_target="tpu_custom_call" | custom-call | flops 20000000000 | bytes 10485760 | tf_op jit(solution)/shard_map/fine/pallas_call | solution.py:219
  87.1 0.0 all-to-all-done
  87.1 0.0 copy-start.1
  87.2 1.0 copy-done.1
  88.1 10.4 %coarse.1 = f32[216,512]{1,0:T(8,128)} custom-call(s32[1]{0:T(128)} %bitcast.core, s32[64,128]{1,0:T(8,128)} %reshape_transpose_reshape.3.src_ref, bf16[4,216,216]{2,1,0:T(8,128)(2,1)} %refs_0_.3, bf16[4,216,216]{2,1,0:T(8,128)(2,1)} %copy-done.4, bf16[4,216,216]{2,1,0:T(8,128)(2,1)} %copy-done.5, bf16[4,216,216]{2,1,0:T(8,128)(2,1)} %collective-permute-done.2.refs_3_, ...), custom_call_target="tpu_custom_call" | custom-call | flops 6000000000 | bytes 10485760 | tf_op jit(solution)/shard_map/coarse/pallas_call | solution.py:219
  (4 shorter events, 0.1 us)
Async XLA Ops:
  0.6 5.8 %copy-start = (s32[2,64]{1,0:T(2,128)S(1)}, s32[2,64]{1,0:T(2,128)}, u32[]{:S(2)}) copy-start(s32[2,64]{1,0:T(2,128)} %param.15) | copy-start | bytes 1540
  1.7 48.0 %collective-permute-start = (bf16[4,216,216]{2,1,0:T(8,128)(2,1)S(1)}, bf16[4,216,216]{2,1,0:T(8,128)(2,1)S(1)}, u32[]{:S(2)}, u32[]{:S(2)}) collective-permute-start(bf16[4,216,216]{2,1,0:T(8,128)(2,1)S(1)} %broadcast_select_fusion), channel_id=1, source_target_pairs={{1,0},{2,1},{3,2},{0,3},{5,4},{6,5},{7,6},{4,7},{9,8},{10,9},{11,1... | collective-permute-start | bytes 1119752 | tf_op jit(solution)/shard_map/ppermute | solution.py:247
  5.4 45.0 %collective-permute-start.1 = (bf16[4,216,216]{2,1,0:T(8,128)(2,1)S(1)}, bf16[4,216,216]{2,1,0:T(8,128)(2,1)S(1)}, u32[]{:S(2)}, u32[]{:S(2)}) collective-permute-start(bf16[4,216,216]{2,1,0:T(8,128)(2,1)S(1)} %broadcast_select_fusion), channel_id=1, source_target_pairs={{2,0},{3,1},{0,2},{1,3},{6,4},{7,5},{4,6},{5,7},{10,8},{11,9},{8,1... | collective-permute-start | bytes 1119752 | tf_op jit(solution)/shard_map/ppermute | solution.py:247
  5.7 44.7 %collective-permute-start.2 = (bf16[4,216,216]{2,1,0:T(8,128)(2,1)S(1)}, bf16[4,216,216]{2,1,0:T(8,128)(2,1)}, u32[]{:S(2)}, u32[]{:S(2)}) collective-permute-start(bf16[4,216,216]{2,1,0:T(8,128)(2,1)S(1)} %broadcast_select_fusion), channel_id=1, source_target_pairs={{3,0},{0,1},{1,2},{2,3},{7,4},{4,5},{5,6},{6,7},{11,8},{8,9},{9,10... | collective-permute-start | bytes 1119752 | tf_op jit(solution)/shard_map/ppermute | solution.py:247
  8.0 17.9 %copy-start.2 = (s32[1024,1]{0,1:T(1,128)S(1)}, s32[1024,1]{0,1:T(1,128)}, u32[]{:S(2)}) copy-start(s32[1024,1]{0,1:T(1,128)} %param.16) | copy-start | bytes 12292
  19.3 34.1 %collective-permute-start.6 = (bf16[4096,128]{1,0:T(8,128)(2,1)}, bf16[4096,128]{1,0:T(8,128)(2,1)S(1)}, u32[]{:S(2)}, u32[]{:S(2)}) collective-permute-start(bf16[4096,128]{1,0:T(8,128)(2,1)} %get-tuple-element.9), channel_id=1, source_target_pairs={{0,4},{4,8},{8,12},{12,16},{16,20},{20,24},{24,28},{28,32},{32,36}... | collective-permute-start | bytes 3145736 | tf_op jit(solution)/shard_map/ppermute | solution.py:242
  23.8 29.6 %collective-permute-start.7 = (bf16[4096,128]{1,0:T(8,128)(2,1)}, bf16[4096,128]{1,0:T(8,128)(2,1)}, u32[]{:S(2)}, u32[]{:S(2)}) collective-permute-start(bf16[4096,128]{1,0:T(8,128)(2,1)} %get-tuple-element.10), channel_id=1, source_target_pairs={{4,0},{8,4},{12,8},{16,12},{20,16},{24,20},{28,24},{32,28},{36,32}... | collective-permute-start | bytes 3145736 | tf_op jit(solution)/shard_map/ppermute | solution.py:242
  35.8 51.3 %all-to-all-start = ((bf16[64,64,128]{2,1,0:T(8,128)(2,1)}), bf16[64,64,128]{2,1,0:T(8,128)(2,1)S(1)}, u32[]{:S(2)}, u32[]{:S(2)}) async-start(bf16[64,64,128]{2,1,0:T(8,128)(2,1)} %bitcast.11), calls=%async_computation | async-start | bytes 2097152 | tf_op jit(solution)/shard_map/all_to_all | solution.py:290
  49.8 3.6 %copy-start.4 = (bf16[4,216,216]{2,1,0:T(8,128)(2,1)}, bf16[4,216,216]{2,1,0:T(8,128)(2,1)S(1)}, u32[]{:S(2)}) copy-start(bf16[4,216,216]{2,1,0:T(8,128)(2,1)S(1)} %collective-permute-done.refs_1_) | copy-start | bytes 1119748
  49.8 3.3 %collective-permute-start.3 = (bf16[4,216,216]{2,1,0:T(8,128)(2,1)S(1)}, bf16[4,216,216]{2,1,0:T(8,128)(2,1)}, u32[]{:S(2)}, u32[]{:S(2)}) collective-permute-start(bf16[4,216,216]{2,1,0:T(8,128)(2,1)S(1)} %collective-permute-done.refs_1_), channel_id=1, source_target_pairs={{4,0},{0,4},{12,8},{8,12},{20,16},{16,20},{28,24},{24,28},{36,32},... | collective-permute-start | bytes 1119752 | tf_op jit(solution)/shard_map/ppermute | solution.py:251
  50.3 3.0 %copy-start.5 = (bf16[4,216,216]{2,1,0:T(8,128)(2,1)}, bf16[4,216,216]{2,1,0:T(8,128)(2,1)S(1)}, u32[]{:S(2)}) copy-start(bf16[4,216,216]{2,1,0:T(8,128)(2,1)S(1)} %collective-permute-done.1.refs_2_) | copy-start | bytes 1119748
  50.3 2.8 %collective-permute-start.4 = (bf16[4,216,216]{2,1,0:T(8,128)(2,1)S(1)}, bf16[4,216,216]{2,1,0:T(8,128)(2,1)}, u32[]{:S(2)}, u32[]{:S(2)}) collective-permute-start(bf16[4,216,216]{2,1,0:T(8,128)(2,1)S(1)} %collective-permute-done.1.refs_2_), channel_id=1, source_target_pairs={{4,0},{0,4},{12,8},{8,12},{20,16},{16,20},{28,24},{24,28},{36,32},... | collective-permute-start | bytes 1119752 | tf_op jit(solution)/shard_map/ppermute | solution.py:251
  50.5 2.9 %collective-permute-start.5 = (bf16[4,216,216]{2,1,0:T(8,128)(2,1)}, bf16[4,216,216]{2,1,0:T(8,128)(2,1)}, u32[]{:S(2)}, u32[]{:S(2)}) collective-permute-start(bf16[4,216,216]{2,1,0:T(8,128)(2,1)} %collective-permute-done.2.refs_3_), channel_id=1, source_target_pairs={{4,0},{0,4},{12,8},{8,12},{20,16},{16,20},{28,24},{24,28},{36,32},... | collective-permute-start | bytes 1119752 | tf_op jit(solution)/shard_map/ppermute | solution.py:251
  53.4 1.0 %copy-start.3 = (bf16[4096,128]{1,0:T(8,128)(2,1)}, bf16[4096,128]{1,0:T(8,128)(2,1)S(1)}, u32[]{:S(2)}) copy-start(bf16[4096,128]{1,0:T(8,128)(2,1)S(1)} %collective-permute-done.6.refs_8_) | copy-start | bytes 3145732
  87.1 1.0 copy-start.1

commit v3 on v2

--- a/solution.py
+++ b/solution.py
@@ -27,44 +27,49 @@
     return lax.dot_general(a, b, (((1,), (1,)), ((), ())), preferred_element_type=jnp.float32)
 
 
-def rows_body(picks, x_hbm, rows_hbm, down, up, x, spread, stage, rows, sent, xsem, osem):
+def spread_matrix():
+    r = lax.broadcasted_iota(jnp.int32, (2 * LANES, 2 * LANES), 0)
+    c = lax.broadcasted_iota(jnp.int32, (2 * LANES, 2 * LANES), 1)
+    return jnp.where(r == 2 * (c % LANES) + c // LANES, 1.0, 0.0).astype(jnp.bfloat16)
+
+
+def column_loads(x_hbm, x, sem):
     chunk = LEAVES // CHUNKS
     loads = []
     for k in range(CHUNKS):
         part = (slice(None), pl.ds(k * chunk, chunk))
-        loads.append(pltpu.make_async_copy(x_hbm.at[part], x.at[part], xsem.at[k]))
-        loads[k].start()
-    r = lax.broadcasted_iota(jnp.int32, (2 * LANES, 2 * LANES), 0)
-    c = lax.broadcasted_iota(jnp.int32, (2 * LANES, 2 * LANES), 1)
-    spread[...] = jnp.where(r == 2 * (c % LANES) + c // LANES, 1.0, 0.0).astype(jnp.bfloat16)
+        loads.append(pltpu.make_async_copy(x_hbm.at[part], x.at[part], sem.at[k]))
+    return loads
+
+
+def columns_to_rows(x, spread, rows, k):
+    chunk = LEAVES // CHUNKS
+    empty = jnp.zeros((2 * LANES - COEFFS, LANES), jnp.bfloat16)
+    for b in range(k * chunk // BLOCK, (k + 1) * chunk // BLOCK):
+        halves = []
+        for start in (b * BLOCK, b * BLOCK + LANES):
+            cols = slice(start, start + LANES)
+            high = jnp.concatenate([x[LANES:COEFFS, cols], empty], axis=0)
+            halves.append(jnp.concatenate([x[0:LANES, cols], high], axis=1))
+        both = contract_lanes(spread[...], jnp.concatenate(halves, axis=0))
+        for h in range(2):
+            rows[pl.ds((2 * b + h) * BLOCK, BLOCK)] = both[:, h * LANES : (h + 1) * LANES]
+
+
+def rows_body(picks, x_hbm, down, up, x, spread, rows, sent, xsem):
+    loads = column_loads(x_hbm, x, xsem)
+    for load in loads:
+        load.start()
+    spread[...] = spread_matrix()
     rows[pl.ds(2 * LEAVES, 2 * TAIL)] = jnp.zeros((2 * TAIL, LANES), jnp.float32)
-    empty = jnp.zeros((2 * LANES - COEFFS, LANES), jnp.bfloat16)
-
-    keeps = []
     for k in range(CHUNKS):
         loads[k].wait()
-        for b in range(k * chunk // BLOCK, (k + 1) * chunk // BLOCK):
-            halves = []
-            for start in (b * BLOCK, b * BLOCK + LANES):
-                cols = slice(start, start + LANES)
-                high = jnp.concatenate([x[LANES:COEFFS, cols], empty], axis=0)
-                halves.append(jnp.concatenate([x[0:LANES, cols], high], axis=1))
-            both = contract_lanes(spread[...], jnp.concatenate(halves, axis=0))
-            for h in range(2):
-                here = pl.ds((2 * b + h) * BLOCK, BLOCK)
-                rows[here] = both[:, h * LANES : (h + 1) * LANES]
-                stage[here] = both[:, h * LANES : (h + 1) * LANES].astype(jnp.bfloat16)
-        here = pl.ds(k * 2 * chunk, 2 * chunk)
-        keeps.append(pltpu.make_async_copy(stage.at[here], rows_hbm.at[here], osem.at[k]))
-        keeps[k].start()
-
+        columns_to_rows(x, spread, rows, k)
     for d, out in enumerate((down, up)):
         for g in range(GHOST):
             f = d * GHOST + g
             sent[g] = rows[pl.ds(picks[f // LANES, f % LANES], 2), :]
         out[...] = sent.reshape(2 * GHOST, LANES)[...].astype(jnp.bfloat16)
-    for keep in keeps:
-        keep.wait()
 
 
 def leaf_rows(multipoles, picks):
@@ -73,15 +78,13 @@
         rows_body,
         name="leaf_rows",
         in_specs=[SMEM, ANY],
-        out_specs=[ANY, VMEM, VMEM],
-        out_shape=[jax.ShapeDtypeStruct((2 * LEAVES, LANES), jnp.bfloat16), ghosts, ghosts],
+        out_specs=[VMEM, VMEM],
+        out_shape=[ghosts, ghosts],
         scratch_shapes=[
             pltpu.VMEM((COEFFS, LEAVES), jnp.bfloat16),
             pltpu.VMEM((2 * LANES, 2 * LANES), jnp.bfloat16),
-            pltpu.VMEM((2 * LEAVES, LANES), jnp.bfloat16),
             pltpu.VMEM((2 * (LEAVES + TAIL), LANES), jnp.float32),
             pltpu.VMEM((GHOST, 2, LANES), jnp.float32),
-            pltpu.SemaphoreType.DMA((CHUNKS,)),
             pltpu.SemaphoreType.DMA((CHUNKS,)),
         ],
         compiler_params=pltpu.CompilerParams(vmem_limit_bytes=60 << 20),
@@ -95,9 +98,11 @@
     for k in range(groups):
         part = (slice(None), pl.ds(k * GROUP, GROUP))
         loads.append(pltpu.make_async_copy(x_hbm.at[part], x.at[part], xsem.at[k]))
-        loads[k].start()
     weights = pltpu.make_async_copy(w_hbm, w, wsem)
+    loads[0].start()
     weights.start()
+    for load in loads[1:]:
+        load.start()
     placed[...] = jnp.zeros_like(placed)
     per_block = BLOCK // 8
     r = lax.broadcasted_iota(jnp.int32, (BLOCK, BLOCK), 0)
@@ -149,28 +154,32 @@
     )(place, multipoles, weights)
 
 
-def translate(name, sources, which_core, weights, swapped, parts, gflops):
+def translate(name, sources, which_core, weights, swapped, multipoles, parts, gflops):
     targets = sources.shape[1]
     tiles = targets // TILE
     n = len(parts)
     width = OPS * TILE // LANES
     src = sources.reshape(OPS, tiles, TILE).swapaxes(0, 1).reshape(tiles * width, LANES)
-    sizes = [p.shape[0] for p in parts]
-    starts = [sum(sizes[:k]) for k in range(n)]
-    slots = sum(sizes)
-    piece = 2048
-    pieces = [(k, at) for k in range(n) for at in range(0, sizes[k], piece)]
+    leaves = [] if multipoles is None else [multipoles]
+    starts = [2 * LEAVES * len(leaves)]
+    for p in parts:
+        starts.append(starts[-1] + p.shape[0])
+    slots = starts[-1]
 
     def body(core, src_ref, *refs):
         here, mine, other = refs[0], refs[1:4], refs[4:7]
         refs = refs[7:]
         part_refs = refs[:n]
-        out = refs[n]
-        stage, buf, z, raw, w, psem, wsem = refs[n + 1 :]
-        copies = []
-        for j, (k, at) in enumerate(pieces):
-            into = stage.at[pl.ds(starts[k] + at, piece)]
-            copies.append(pltpu.make_async_copy(part_refs[k].at[pl.ds(at, piece)], into, psem.at[j]))
+        refs = refs[n:]
+        x_hbm = refs[: len(leaves)]
+        refs = refs[len(leaves) :]
+        out, buf, z, raw, w, wsem = refs[:6]
+        loads = []
+        if leaves:
+            x, spread, xsem = refs[6:]
+            loads = column_loads(x_hbm[0], x, xsem)
+            for load in loads:
+                load.start()
 
         pltpu.make_async_copy(here, raw.at[pl.ds(0, 4)], wsem.at[0]).start()
         for q in range(3):
@@ -184,8 +193,14 @@
             def _():
                 pltpu.make_async_copy(other[q], into, wsem.at[q + 1]).start()
 
-        for copy in copies:
-            copy.start()
+        buf[pl.ds(slots, 2 * TAIL)] = jnp.zeros((2 * TAIL, LANES), jnp.float32)
+        for k in range(n):
+            buf[pl.ds(starts[k], starts[k + 1] - starts[k])] = part_refs[k][...].astype(jnp.float32)
+        if leaves:
+            spread[...] = spread_matrix()
+            for k in range(CHUNKS):
+                loads[k].wait()
+                columns_to_rows(x, spread, buf, k)
         for q in range(4):
             pltpu.make_async_copy(here, raw.at[pl.ds(4 * q, 4)], wsem.at[q]).wait()
         r = lax.broadcasted_iota(jnp.int32, (2 * LANES, COEFFS), 0)
@@ -193,12 +208,6 @@
         unit = jnp.where(r == c, 1.0, 0.0).astype(jnp.bfloat16)
         for o in range(OPS):
             w[o * 2 * LANES : (o + 1) * 2 * LANES] = contract_lanes(unit, raw[o]).astype(jnp.bfloat16)
-
-        buf[pl.ds(slots, 2 * TAIL)] = jnp.zeros((2 * TAIL, LANES), jnp.float32)
-        for copy, (k, at) in zip(copies, pieces):
-            copy.wait()
-            now = pl.ds(starts[k] + at, piece)
-            buf[now] = stage[now].astype(jnp.float32)
 
         @pl.loop(0, tiles)
         def _(tile):
@@ -219,21 +228,25 @@
     return pl.pallas_call(
         body,
         name=name,
-        in_specs=[SMEM, SMEM] + [ANY] * (7 + n),
+        in_specs=[SMEM, SMEM] + [ANY] * 7 + [VMEM] * n + [ANY] * len(leaves),
         out_specs=VMEM,
         out_shape=jax.ShapeDtypeStruct((COEFFS, targets), jnp.float32),
         scratch_shapes=[
-            pltpu.VMEM((slots, LANES), jnp.bfloat16),
             pltpu.VMEM((slots + 2 * TAIL, LANES), jnp.float32),
             pltpu.VMEM((OPS, TILE, 2, LANES), jnp.float32),
             pltpu.VMEM((OPS, COEFFS, COEFFS), jnp.bfloat16),
             pltpu.VMEM((OPS * 2 * LANES, COEFFS), jnp.bfloat16),
-            pltpu.SemaphoreType.DMA((len(pieces),)),
             pltpu.SemaphoreType.DMA((4,)),
-        ],
+        ]
+        + [
+            pltpu.VMEM((COEFFS, LEAVES), jnp.bfloat16),
+            pltpu.VMEM((2 * LANES, 2 * LANES), jnp.bfloat16),
+            pltpu.SemaphoreType.DMA((CHUNKS,)),
+        ]
+        * len(leaves),
         compiler_params=pltpu.CompilerParams(vmem_limit_bytes=60 << 20),
         cost_estimate=pl.CostEstimate(flops=gflops * 1_000_000_000, bytes_accessed=10 << 20, transcendentals=0),
-    )(which_core, src, *weights, *parts)
+    )(which_core, src, *weights, *parts, *leaves)
 
 
 def passed_along(block, axis, distance):
@@ -273,7 +286,7 @@
     count_here = lax.dynamic_slice_in_dim(ghost_count, slab_here, 1, 1)
     inside = jnp.arange(GHOST, dtype=jnp.int32)[None, :] < count_here
     picks = jnp.where(inside, 2 * index_here, 2 * LEAVES).reshape(2 * GHOST // LANES, LANES)
-    rows, down, up = leaf_rows(multipoles, picks)
+    down, up = leaf_rows(multipoles, picks)
     upper = passed_along(down, "slab", -1)
     lower = passed_along(up, "slab", 1)
 
@@ -285,7 +298,7 @@
     rank = jnp.sum(before * matches.astype(jnp.float32), axis=1).astype(jnp.int32)
     capacity = SLOTS // slab_count
     place = (2 * (owners * capacity + rank)).reshape(PARENTS // LANES, LANES)
-    place, rows = lax.optimization_barrier((place, rows))
+    place, down = lax.optimization_barrier((place, down))
     outgoing = placed_parents(multipoles, m2m, place)
     received = lax.all_to_all(
         outgoing.reshape(slab_count, 2 * capacity, LANES), "slab", split_axis=0, concat_axis=0, tiled=True
@@ -297,7 +310,8 @@
         core_flag,
         [fine_m2l, *mine, *other],
         1,
-        [rows, lower, upper],
+        multipoles,
+        [lower, upper],
         20,
     )
     coarse_local = translate(
@@ -306,6 +320,7 @@
         core_flag,
         [coarse_m2l, *mine, *other],
         0,
+        None,
         [received],
         6,
     )

time: 99.4 us -> 97 us (0.976)
  Pallas kernels: 63.1 us -> 59.4 us
  starting transfers between devices: 25.3 us -> 26.3 us
    pallas_call x1, Pallas kernels: 11.3 us -> 8.51 us  [leaf_rows(): pl.pallas_call(rows_body, name='leaf_rows', in_specs=[SMEM, ANY], out_spe...]
    ppermute x3, starting transfers between devices: 4.68 us -> 5.89 us  [turned(): lax.ppermute(block, 'lvl', [((i + distance) % size, i) for i in range(siz...]
  transfers between devices with their start and end apart: 9 -> 9, of which waited for: 2 -> 2; matrix products, arithmetic and copies ran while one was open for 6% -> 6% of each run, Pallas kernels for 53% -> 51%
where the time goes in v3:
time: 97 us; the launch traced here: 96.4 us
  Pallas kernels  59.4 us (61%)
  starting transfers between devices  26.3 us (27%)
  other arithmetic  4.22 us (4%)
  local copies, waits for them, and re-layouts  4.16 us (4%)
    pallas_call x2, Pallas kernels, translate(): pl.pallas_call(body, name=name, in_specs=[SMEM, SMEM] + [ANY] * 7 + [VMEM...  42.4 us
    all_to_all x1, starting transfers between devices, per_device(): lax.all_to_all(outgoing.reshape(slab_count, 2 * capacity, LANES), 'slab',...  13 us
    pallas_call x1, Pallas kernels, leaf_rows(): pl.pallas_call(rows_body, name='leaf_rows', in_specs=[SMEM, ANY], out_spe...  8.51 us
    pallas_call x1, Pallas kernels, placed_parents(): pl.pallas_call(parents_body, name='placed_parents', in_specs=[SMEM, ANY,...  8.44 us
    ppermute x2, starting transfers between devices, passed_along(): return lax.ppermute(block, axis, route)  6.47 us
    ppermute x3, starting transfers between devices, turned(): lax.ppermute(block, 'lvl', [((i + distance) % size, i) for i in range(siz...  5.89 us
    unnamed x12, local copies, waits for them, and re-layouts  1.95 us
  transfers between devices with their start and end apart: 9, of which 2 were waited for; matrix products, arithmetic and copies ran while one was open for 6% of the time, Pallas kernels for 51%

profile of v3, /device:TPU:1, one launch (start us, length us, event | category | flops | bytes accessed | tf_op | source)
XLA Modules:
  0.0 96.4 jit_solution(2737449084148217788)
XLA Ops:
  0.6 0.0 copy-start
  0.7 1.1 %broadcast_select_fusion = bf16[4,216,216]{2,1,0:T(8,128)(2,1)S(1)} fusion(bf16[4,216,216]{2,1,0:T(8,128)(2,1)} %refs_0_.2, bf16[4,216,216]{2,1,0:T(8,128)(2,1)} %refs_0_.3, pred[]{:T(512)S(6)} %eq.20), kind=kLoop, calls=%fused_computation.4 | loop fusion | flops 186624 | bytes 1119745 | tf_op jit(solution)/shard_map/jit(_where)/select_n | solution.py:280
  1.7 2.2 %collective-permute-start.2 = (bf16[4,216,216]{2,1,0:T(8,128)(2,1)S(1)}, bf16[4,216,216]{2,1,0:T(8,128)(2,1)S(1)}, u32[]{:S(2)}, u32[]{:S(2)}) collective-permute-start(bf16[4,216,216]{2,1,0:T(8,128)(2,1)S(1)} %broadcast_select_fusion), channel_id=1, source_target_pairs={{3,0},{0,1},{1,2},{2,3},{7,4},{4,5},{5,6},{6,7},{11,8},{8,9},{9,10... | collective-permute-start | bytes 1119752 | tf_op jit(solution)/shard_map/ppermute | solution.py:260
  3.9 2.6 %collective-permute-start.1 = (bf16[4,216,216]{2,1,0:T(8,128)(2,1)S(1)}, bf16[4,216,216]{2,1,0:T(8,128)(2,1)S(1)}, u32[]{:S(2)}, u32[]{:S(2)}) collective-permute-start(bf16[4,216,216]{2,1,0:T(8,128)(2,1)S(1)} %broadcast_select_fusion), channel_id=1, source_target_pairs={{2,0},{3,1},{0,2},{1,3},{6,4},{7,5},{4,6},{5,7},{10,8},{11,9},{8,1... | collective-permute-start | bytes 1119752 | tf_op jit(solution)/shard_map/ppermute | solution.py:260
  6.6 1.1 %collective-permute-start = (bf16[4,216,216]{2,1,0:T(8,128)(2,1)S(1)}, bf16[4,216,216]{2,1,0:T(8,128)(2,1)}, u32[]{:S(2)}, u32[]{:S(2)}) collective-permute-start(bf16[4,216,216]{2,1,0:T(8,128)(2,1)S(1)} %broadcast_select_fusion), channel_id=1, source_target_pairs={{1,0},{2,1},{3,2},{0,3},{5,4},{6,5},{7,6},{4,7},{9,8},{10,9},{11,1... | collective-permute-start | bytes 1119752 | tf_op jit(solution)/shard_map/ppermute | solution.py:260
  7.6 0.0 copy-done
  7.6 0.2 fusion.8
  7.8 0.8 compare_select_fusion
  8.6 0.6 reshape.31.picks
  9.2 0.0 copy-start.2
  9.2 8.5 %leaf_rows.1 = (bf16[4096,128]{1,0:T(8,128)(2,1)}, bf16[4096,128]{1,0:T(8,128)(2,1)}) custom-call(s32[32,128]{1,0:T(8,128)} %reshape.31.picks, bf16[216,8192]{1,0:T(8,128)(2,1)} %x_hbm.3), custom_call_target="tpu_custom_call" | custom-call | flops 6000000000 | bytes 10485760 | tf_op jit(solution)/shard_map/leaf_rows/pallas_call | solution.py:77
  17.8 4.5 %collective-permute-start.6 = (bf16[4096,128]{1,0:T(8,128)(2,1)}, bf16[4096,128]{1,0:T(8,128)(2,1)S(1)}, u32[]{:S(2)}, u32[]{:S(2)}) collective-permute-start(bf16[4096,128]{1,0:T(8,128)(2,1)} %get-tuple-element.5), channel_id=1, source_target_pairs={{0,4},{4,8},{8,12},{12,16},{16,20},{20,24},{24,28},{28,32},{32,36}... | collective-permute-start | bytes 3145736 | tf_op jit(solution)/shard_map/ppermute | solution.py:255
  22.3 1.9 %collective-permute-start.7 = (bf16[4096,128]{1,0:T(8,128)(2,1)}, bf16[4096,128]{1,0:T(8,128)(2,1)}, u32[]{:S(2)}, u32[]{:S(2)}) collective-permute-start(bf16[4096,128]{1,0:T(8,128)(2,1)} %get-tuple-element.6), channel_id=1, source_target_pairs={{4,0},{8,4},{12,8},{16,12},{20,16},{24,20},{28,24},{32,28},{36,32}... | collective-permute-start | bytes 3145736 | tf_op jit(solution)/shard_map/ppermute | solution.py:255
  24.2 0.0 copy-done.2
  24.3 0.6 fusion.2
  24.9 0.6 fusion.7.place
  25.5 8.4 %placed_parents.1 = bf16[4096,128]{1,0:T(8,128)(2,1)} custom-call(s32[8,128]{1,0:T(8,128)} %fusion.7.place, bf16[216,8192]{1,0:T(8,128)(2,1)} %x_hbm.3, bf16[8,216,216]{2,1,0:T(8,128)(2,1)} %w_hbm.1), custom_call_target="tpu_custom_call" | custom-call | flops 4000000000 | bytes 6291456 | tf_op jit(solution)/shard_map/placed_parents/pallas_call | solution.py:137
  33.9 13.0 %all-to-all-start = ((bf16[64,64,128]{2,1,0:T(8,128)(2,1)}), bf16[64,64,128]{2,1,0:T(8,128)(2,1)S(1)}, u32[]{:S(2)}, u32[]{:S(2)}) async-start(bf16[64,64,128]{2,1,0:T(8,128)(2,1)} %bitcast.11), calls=%async_computation | async-start | bytes 2097152 | tf_op jit(solution)/shard_map/all_to_all | solution.py:303
  46.9 0.8 dynamic-slice_multiply_fusion.1
  47.7 0.6 reshape_transpose_reshape.3.src_ref
  48.3 0.0 collective-permute-done.2.refs_3_
  48.3 0.0 copy-start.4
  48.3 0.5 collective-permute-start.5
  48.8 0.0 collective-permute-done.1.refs_2_
  48.8 0.0 copy-start.5
  48.8 0.1 collective-permute-start.4
  48.9 0.0 collective-permute-done.refs_1_
  48.9 0.4 collective-permute-start.3
  49.3 0.9 dynamic-slice_multiply_fusion
  50.3 0.1 reshape.29
  50.4 0.7 reshape.30.src_ref
  51.1 0.0 collective-permute-done.5.refs_6_
  51.1 0.5 collective-permute-done.4.refs_5_
  51.6 0.2 collective-permute-done.3.refs_4_
  51.8 0.0 collective-permute-done.6.refs_7_
  51.8 0.0 copy-start.3
  51.8 0.0 collective-permute-done.7.refs_8_
  51.8 0.0 copy-done.4
  51.8 0.0 copy-done.5
  51.8 1.0 %copy-done.3 = bf16[4096,128]{1,0:T(8,128)(2,1)} copy-done((bf16[4096,128]{1,0:T(8,128)(2,1)}, bf16[4096,128]{1,0:T(8,128)(2,1)S(1)}, u32[]{:S(2)}) %copy-start.3) | copy-done | bytes 1048600
  52.8 32.3 %fine.1 = f32[216,2048]{1,0:T(8,128)} custom-call(s32[1]{0:T(128)} %bitcast.core, s32[256,128]{1,0:T(8,128)} %reshape.30.src_ref, bf16[4,216,216]{2,1,0:T(8,128)(2,1)} %refs_0_.2, bf16[4,216,216]{2,1,0:T(8,128)(2,1)} %collective-permute-done.refs_1_, bf16[4,216,216]{2,1,0:T(8,128)(2,1)} %copy-done.5, bf16[4,216,216]{2,1,0:T(8,128)(2,1)} %copy-done.4, ...), custom_call_target="tpu_custom_call" | custom-call | flops 20000000000 | bytes 10485760 | tf_op jit(solution)/shard_map/fine/pallas_call | solution.py:228
  85.1 0.0 all-to-all-done
  85.1 0.0 copy-start.1
  85.1 1.0 copy-done.1
  86.0 10.2 %coarse.1 = f32[216,512]{1,0:T(8,128)} custom-call(s32[1]{0:T(128)} %bitcast.core, s32[64,128]{1,0:T(8,128)} %reshape_transpose_reshape.3.src_ref, bf16[4,216,216]{2,1,0:T(8,128)(2,1)} %refs_0_.3, bf16[4,216,216]{2,1,0:T(8,128)(2,1)} %collective-permute-done.refs_1_, bf16[4,216,216]{2,1,0:T(8,128)(2,1)} %copy-done.5, bf16[4,216,216]{2,1,0:T(8,128)(2,1)} %copy-done.4, ...), custom_call_target="tpu_custom_call" | custom-call | flops 6000000000 | bytes 10485760 | tf_op jit(solution)/shard_map/coarse/pallas_call | solution.py:228
  (4 shorter events, 0.1 us)
Async XLA Ops:
  0.6 7.0 %copy-start = (s32[2,64]{1,0:T(2,128)S(1)}, s32[2,64]{1,0:T(2,128)}, u32[]{:S(2)}) copy-start(s32[2,64]{1,0:T(2,128)} %param.15) | copy-start | bytes 1540
  1.7 46.6 %collective-permute-start.2 = (bf16[4,216,216]{2,1,0:T(8,128)(2,1)S(1)}, bf16[4,216,216]{2,1,0:T(8,128)(2,1)S(1)}, u32[]{:S(2)}, u32[]{:S(2)}) collective-permute-start(bf16[4,216,216]{2,1,0:T(8,128)(2,1)S(1)} %broadcast_select_fusion), channel_id=1, source_target_pairs={{3,0},{0,1},{1,2},{2,3},{7,4},{4,5},{5,6},{6,7},{11,8},{8,9},{9,10... | collective-permute-start | bytes 1119752 | tf_op jit(solution)/shard_map/ppermute | solution.py:260
  3.9 44.8 %collective-permute-start.1 = (bf16[4,216,216]{2,1,0:T(8,128)(2,1)S(1)}, bf16[4,216,216]{2,1,0:T(8,128)(2,1)S(1)}, u32[]{:S(2)}, u32[]{:S(2)}) collective-permute-start(bf16[4,216,216]{2,1,0:T(8,128)(2,1)S(1)} %broadcast_select_fusion), channel_id=1, source_target_pairs={{2,0},{3,1},{0,2},{1,3},{6,4},{7,5},{4,6},{5,7},{10,8},{11,9},{8,1... | collective-permute-start | bytes 1119752 | tf_op jit(solution)/shard_map/ppermute | solution.py:260
  6.6 42.3 %collective-permute-start = (bf16[4,216,216]{2,1,0:T(8,128)(2,1)S(1)}, bf16[4,216,216]{2,1,0:T(8,128)(2,1)}, u32[]{:S(2)}, u32[]{:S(2)}) collective-permute-start(bf16[4,216,216]{2,1,0:T(8,128)(2,1)S(1)} %broadcast_select_fusion), channel_id=1, source_target_pairs={{1,0},{2,1},{3,2},{0,3},{5,4},{6,5},{7,6},{4,7},{9,8},{10,9},{11,1... | collective-permute-start | bytes 1119752 | tf_op jit(solution)/shard_map/ppermute | solution.py:260
  9.2 15.0 %copy-start.2 = (s32[1024,1]{0,1:T(1,128)S(1)}, s32[1024,1]{0,1:T(1,128)}, u32[]{:S(2)}) copy-start(s32[1024,1]{0,1:T(1,128)} %param.16) | copy-start | bytes 12292
  17.8 34.0 %collective-permute-start.6 = (bf16[4096,128]{1,0:T(8,128)(2,1)}, bf16[4096,128]{1,0:T(8,128)(2,1)S(1)}, u32[]{:S(2)}, u32[]{:S(2)}) collective-permute-start(bf16[4096,128]{1,0:T(8,128)(2,1)} %get-tuple-element.5), channel_id=1, source_target_pairs={{0,4},{4,8},{8,12},{12,16},{16,20},{20,24},{24,28},{28,32},{32,36}... | collective-permute-start | bytes 3145736 | tf_op jit(solution)/shard_map/ppermute | solution.py:255
  22.3 29.5 %collective-permute-start.7 = (bf16[4096,128]{1,0:T(8,128)(2,1)}, bf16[4096,128]{1,0:T(8,128)(2,1)}, u32[]{:S(2)}, u32[]{:S(2)}) collective-permute-start(bf16[4096,128]{1,0:T(8,128)(2,1)} %get-tuple-element.6), channel_id=1, source_target_pairs={{4,0},{8,4},{12,8},{16,12},{20,16},{24,20},{28,24},{32,28},{36,32}... | collective-permute-start | bytes 3145736 | tf_op jit(solution)/shard_map/ppermute | solution.py:255
  33.9 51.2 %all-to-all-start = ((bf16[64,64,128]{2,1,0:T(8,128)(2,1)}), bf16[64,64,128]{2,1,0:T(8,128)(2,1)S(1)}, u32[]{:S(2)}, u32[]{:S(2)}) async-start(bf16[64,64,128]{2,1,0:T(8,128)(2,1)} %bitcast.11), calls=%async_computation | async-start | bytes 2097152 | tf_op jit(solution)/shard_map/all_to_all | solution.py:303
  48.3 3.5 %copy-start.4 = (bf16[4,216,216]{2,1,0:T(8,128)(2,1)}, bf16[4,216,216]{2,1,0:T(8,128)(2,1)S(1)}, u32[]{:S(2)}) copy-start(bf16[4,216,216]{2,1,0:T(8,128)(2,1)S(1)} %collective-permute-done.2.refs_3_) | copy-start | bytes 1119748
  48.3 2.8 %collective-permute-start.5 = (bf16[4,216,216]{2,1,0:T(8,128)(2,1)S(1)}, bf16[4,216,216]{2,1,0:T(8,128)(2,1)}, u32[]{:S(2)}, u32[]{:S(2)}) collective-permute-start(bf16[4,216,216]{2,1,0:T(8,128)(2,1)S(1)} %collective-permute-done.2.refs_3_), channel_id=1, source_target_pairs={{4,0},{0,4},{12,8},{8,12},{20,16},{16,20},{28,24},{24,28},{36,32},... | collective-permute-start | bytes 1119752 | tf_op jit(solution)/shard_map/ppermute | solution.py:264
  48.8 3.0 %copy-start.5 = (bf16[4,216,216]{2,1,0:T(8,128)(2,1)}, bf16[4,216,216]{2,1,0:T(8,128)(2,1)S(1)}, u32[]{:S(2)}) copy-start(bf16[4,216,216]{2,1,0:T(8,128)(2,1)S(1)} %collective-permute-done.1.refs_2_) | copy-start | bytes 1119748
  48.8 2.8 %collective-permute-start.4 = (bf16[4,216,216]{2,1,0:T(8,128)(2,1)S(1)}, bf16[4,216,216]{2,1,0:T(8,128)(2,1)}, u32[]{:S(2)}, u32[]{:S(2)}) collective-permute-start(bf16[4,216,216]{2,1,0:T(8,128)(2,1)S(1)} %collective-permute-done.1.refs_2_), channel_id=1, source_target_pairs={{4,0},{0,4},{12,8},{8,12},{20,16},{16,20},{28,24},{24,28},{36,32},... | collective-permute-start | bytes 1119752 | tf_op jit(solution)/shard_map/ppermute | solution.py:264
  48.9 2.9 %collective-permute-start.3 = (bf16[4,216,216]{2,1,0:T(8,128)(2,1)}, bf16[4,216,216]{2,1,0:T(8,128)(2,1)}, u32[]{:S(2)}, u32[]{:S(2)}) collective-permute-start(bf16[4,216,216]{2,1,0:T(8,128)(2,1)} %collective-permute-done.refs_1_), channel_id=1, source_target_pairs={{4,0},{0,4},{12,8},{8,12},{20,16},{16,20},{28,24},{24,28},{36,32},... | collective-permute-start | bytes 1119752 | tf_op jit(solution)/shard_map/ppermute | solution.py:264
  51.8 1.0 %copy-start.3 = (bf16[4096,128]{1,0:T(8,128)(2,1)}, bf16[4096,128]{1,0:T(8,128)(2,1)S(1)}, u32[]{:S(2)}) copy-start(bf16[4096,128]{1,0:T(8,128)(2,1)S(1)} %collective-permute-done.6.refs_7_) | copy-start | bytes 3145732
  85.1 1.0 %copy-start.1 = (bf16[64,64,128]{2,1,0:T(8,128)(2,1)}, bf16[64,64,128]{2,1,0:T(8,128)(2,1)S(1)}, u32[]{:S(2)}) copy-start(bf16[64,64,128]{2,1,0:T(8,128)(2,1)S(1)} %all-to-all-done) | copy-start | bytes 3145732

commit v4 on v3

--- a/solution.py
+++ b/solution.py
@@ -56,53 +56,17 @@
             rows[pl.ds((2 * b + h) * BLOCK, BLOCK)] = both[:, h * LANES : (h + 1) * LANES]
 
 
-def rows_body(picks, x_hbm, down, up, x, spread, rows, sent, xsem):
+def upward_body(picks, place, x_hbm, w_hbm, down, up, out, *scratch):
+    x, spread, rows, sent, w, children, boxes, placed, xsem, wsem = scratch
     loads = column_loads(x_hbm, x, xsem)
-    for load in loads:
+    weights = pltpu.make_async_copy(w_hbm, w, wsem)
+    for load in loads[:4]:
+        load.start()
+    weights.start()
+    for load in loads[4:]:
         load.start()
     spread[...] = spread_matrix()
     rows[pl.ds(2 * LEAVES, 2 * TAIL)] = jnp.zeros((2 * TAIL, LANES), jnp.float32)
-    for k in range(CHUNKS):
-        loads[k].wait()
-        columns_to_rows(x, spread, rows, k)
-    for d, out in enumerate((down, up)):
-        for g in range(GHOST):
-            f = d * GHOST + g
-            sent[g] = rows[pl.ds(picks[f // LANES, f % LANES], 2), :]
-        out[...] = sent.reshape(2 * GHOST, LANES)[...].astype(jnp.bfloat16)
-
-
-def leaf_rows(multipoles, picks):
-    ghosts = jax.ShapeDtypeStruct((2 * GHOST, LANES), jnp.bfloat16)
-    return pl.pallas_call(
-        rows_body,
-        name="leaf_rows",
-        in_specs=[SMEM, ANY],
-        out_specs=[VMEM, VMEM],
-        out_shape=[ghosts, ghosts],
-        scratch_shapes=[
-            pltpu.VMEM((COEFFS, LEAVES), jnp.bfloat16),
-            pltpu.VMEM((2 * LANES, 2 * LANES), jnp.bfloat16),
-            pltpu.VMEM((2 * (LEAVES + TAIL), LANES), jnp.float32),
-            pltpu.VMEM((GHOST, 2, LANES), jnp.float32),
-            pltpu.SemaphoreType.DMA((CHUNKS,)),
-        ],
-        compiler_params=pltpu.CompilerParams(vmem_limit_bytes=60 << 20),
-        cost_estimate=pl.CostEstimate(flops=6_000_000_000, bytes_accessed=10 << 20, transcendentals=0),
-    )(picks, multipoles)
-
-
-def parents_body(place, x_hbm, w_hbm, out, x, w, children, rows, placed, xsem, wsem):
-    groups = LEAVES // GROUP
-    loads = []
-    for k in range(groups):
-        part = (slice(None), pl.ds(k * GROUP, GROUP))
-        loads.append(pltpu.make_async_copy(x_hbm.at[part], x.at[part], xsem.at[k]))
-    weights = pltpu.make_async_copy(w_hbm, w, wsem)
-    loads[0].start()
-    weights.start()
-    for load in loads[1:]:
-        load.start()
     placed[...] = jnp.zeros_like(placed)
     per_block = BLOCK // 8
     r = lax.broadcasted_iota(jnp.int32, (BLOCK, BLOCK), 0)
@@ -110,9 +74,12 @@
     octant_major = jnp.where(c == (r % per_block) * 8 + r // per_block, 1.0, 0.0).astype(jnp.bfloat16)
     per_group = GROUP // 8
     empty = jnp.zeros((per_group, 2 * LANES - COEFFS), jnp.float32)
-
-    for s in range(groups):
-        loads[s].wait()
+    chunks = CHUNKS * GROUP // LEAVES
+
+    for s in range(LEAVES // GROUP):
+        for k in range(s * chunks, (s + 1) * chunks):
+            loads[k].wait()
+            columns_to_rows(x, spread, rows, k)
         for b in range(GROUP // BLOCK):
             start = s * GROUP + b * BLOCK
             sorted_rows = contract_lanes(octant_major, x[:, start : start + BLOCK]).astype(jnp.bfloat16)
@@ -124,34 +91,43 @@
         for o in range(1, 8):
             total += contract_lanes(children[o], w[o])
         first = s * 2 * per_group
-        rows[pl.ds(first, per_group, 2), :] = total[:, :LANES]
-        rows[pl.ds(first + 1, per_group, 2), :] = jnp.concatenate([total[:, LANES:], empty], axis=1)
-
-    box = rows.reshape(PARENTS, 2, LANES)
+        boxes[pl.ds(first, per_group, 2), :] = total[:, :LANES]
+        boxes[pl.ds(first + 1, per_group, 2), :] = jnp.concatenate([total[:, LANES:], empty], axis=1)
+
+    for d, ghosts in enumerate((down, up)):
+        for g in range(GHOST):
+            f = d * GHOST + g
+            sent[g] = rows[pl.ds(picks[f // LANES, f % LANES], 2), :]
+        ghosts[...] = sent.reshape(2 * GHOST, LANES)[...].astype(jnp.bfloat16)
+    box = boxes.reshape(PARENTS, 2, LANES)
     for p in range(PARENTS):
         placed[pl.ds(place[p // LANES, p % LANES], 2), :] = box[p]
     out[...] = placed[...].astype(jnp.bfloat16)
 
 
-def placed_parents(multipoles, weights, place):
+def upward(multipoles, m2m, picks, place):
+    ghosts = jax.ShapeDtypeStruct((2 * GHOST, LANES), jnp.bfloat16)
     return pl.pallas_call(
-        parents_body,
-        name="placed_parents",
-        in_specs=[SMEM, ANY, ANY],
-        out_specs=VMEM,
-        out_shape=jax.ShapeDtypeStruct((2 * SLOTS, LANES), jnp.bfloat16),
+        upward_body,
+        name="upward",
+        in_specs=[SMEM, SMEM, ANY, ANY],
+        out_specs=[VMEM, VMEM, VMEM],
+        out_shape=[ghosts, ghosts, jax.ShapeDtypeStruct((2 * SLOTS, LANES), jnp.bfloat16)],
         scratch_shapes=[
             pltpu.VMEM((COEFFS, LEAVES), jnp.bfloat16),
+            pltpu.VMEM((2 * LANES, 2 * LANES), jnp.bfloat16),
+            pltpu.VMEM((2 * (LEAVES + TAIL), LANES), jnp.float32),
+            pltpu.VMEM((GHOST, 2, LANES), jnp.float32),
             pltpu.VMEM((8, COEFFS, COEFFS), jnp.bfloat16),
             pltpu.VMEM((8, GROUP // 8, COEFFS), jnp.bfloat16),
             pltpu.VMEM((2 * PARENTS, LANES), jnp.float32),
             pltpu.VMEM((2 * SLOTS, LANES), jnp.float32),
-            pltpu.SemaphoreType.DMA((LEAVES // GROUP,)),
+            pltpu.SemaphoreType.DMA((CHUNKS,)),
             pltpu.SemaphoreType.DMA(()),
         ],
         compiler_params=pltpu.CompilerParams(vmem_limit_bytes=60 << 20),
-        cost_estimate=pl.CostEstimate(flops=4_000_000_000, bytes_accessed=6 << 20, transcendentals=0),
-    )(place, multipoles, weights)
+        cost_estimate=pl.CostEstimate(flops=10_000_000_000, bytes_accessed=8 << 20, transcendentals=0),
+    )(picks, place, multipoles, m2m)
 
 
 def translate(name, sources, which_core, weights, swapped, multipoles, parts, gflops):
@@ -286,10 +262,6 @@
     count_here = lax.dynamic_slice_in_dim(ghost_count, slab_here, 1, 1)
     inside = jnp.arange(GHOST, dtype=jnp.int32)[None, :] < count_here
     picks = jnp.where(inside, 2 * index_here, 2 * LEAVES).reshape(2 * GHOST // LANES, LANES)
-    down, up = leaf_rows(multipoles, picks)
-    upper = passed_along(down, "slab", -1)
-    lower = passed_along(up, "slab", 1)
-
     owners = owner[:, 0]
     matches = (owners[:, None] == jnp.arange(slab_count, dtype=jnp.int32)[None, :]).astype(jnp.bfloat16)
     order = jnp.arange(PARENTS, dtype=jnp.int32)
@@ -298,8 +270,9 @@
     rank = jnp.sum(before * matches.astype(jnp.float32), axis=1).astype(jnp.int32)
     capacity = SLOTS // slab_count
     place = (2 * (owners * capacity + rank)).reshape(PARENTS // LANES, LANES)
-    place, down = lax.optimization_barrier((place, down))
-    outgoing = placed_parents(multipoles, m2m, place)
+    down, up, outgoing = upward(multipoles, m2m, picks, place)
+    upper = passed_along(down, "slab", -1)
+    lower = passed_along(up, "slab", 1)
     received = lax.all_to_all(
         outgoing.reshape(slab_count, 2 * capacity, LANES), "slab", split_axis=0, concat_axis=0, tiled=True
     ).reshape(2 * SLOTS, LANES)

time: 97 us -> 96.8 us (level)
  Pallas kernels: 59.4 us -> 56 us
  waiting for transfers between devices: 0.73 us -> 3.63 us
    ppermute x3, waiting for transfers between devices: 0.01 us -> 3.61 us  [turned(): lax.ppermute(block, 'lvl', [((i + distance) % size, i) for i in range(siz...]
    pallas_call x2 -> x1, Pallas kernels: 17 us -> 13.5 us  [upward(): pl.pallas_call(upward_body, name='upward', in_specs=[SMEM, SMEM, ANY, ANY...]
    ppermute x3, starting transfers between devices: 5.89 us -> 4.08 us  [turned(): lax.ppermute(block, 'lvl', [((i + distance) % size, i) for i in range(siz...]
    select_n x1, other arithmetic: 1.07 us -> 0.05 us  [per_device(): fetched = jnp.where(core == 0, fine_m2l, coarse_m2l)]
    unnamed x12 -> x18, local copies, waits for them, and re-layouts: 1.95 us -> 1.85 us
  transfers between devices with their start and end apart: 9 -> 9, of which waited for: 2 -> 2; matrix products, arithmetic and copies ran while one was open for 6% -> 3% of each run, Pallas kernels for 51% -> 34%
where the time goes in v4:
time: 96.8 us; the launch traced here: 96.3 us
  Pallas kernels  56 us (58%)
  starting transfers between devices  26.4 us (27%)
  local copies, waits for them, and re-layouts  4.08 us (4%)
  other arithmetic  3.87 us (4%)
  waiting for transfers between devices  3.63 us (4%)
  matrix products  1.35 us (1%)
  between operations  1.01 us (1%)
    pallas_call x2, Pallas kernels, translate(): pl.pallas_call(body, name=name, in_specs=[SMEM, SMEM] + [ANY] * 7 + [VMEM...  42.4 us
    all_to_all x1, starting transfers between devices, per_device(): lax.all_to_all(outgoing.reshape(slab_count, 2 * capacity, LANES), 'slab',...  13.8 us
    pallas_call x1, Pallas kernels, upward(): pl.pallas_call(upward_body, name='upward', in_specs=[SMEM, SMEM, ANY, ANY...  13.5 us
    ppermute x2, starting transfers between devices, passed_along(): return lax.ppermute(block, axis, route)  7.42 us
    ppermute x3, starting transfers between devices, turned(): lax.ppermute(block, 'lvl', [((i + distance) % size, i) for i in range(siz...  4.08 us
    ppermute x3, waiting for transfers between devices, turned(): lax.ppermute(block, 'lvl', [((i + distance) % size, i) for i in range(siz...  3.61 us
  transfers between devices with their start and end apart: 9, of which 2 were waited for; matrix products, arithmetic and copies ran while one was open for 3% of the time, Pallas kernels for 34%

profile of v4, /device:TPU:1, one launch (start us, length us, event | category | flops | bytes accessed | tf_op | source)
XLA Modules:
  0.0 96.3 jit_solution(1512074679703989984)
XLA Ops:
  0.6 0.0 copy-start
  0.7 0.7 broadcast_multiply_fusion
  1.3 1.4 %fusion.2 = f32[1024]{0:T(1024)S(1)} fusion(s32[1024]{0:T(1024)} %bitcast.14), kind=kOutput, calls=%fused_computation.3 | convolution fusion | flops 135658496 | bytes 8192 | tf_op jit(solution)/shard_map/dot_general | solution.py:269
  2.7 0.0 copy-done
  2.7 0.2 fusion.8
  2.9 0.8 compare_select_fusion
  3.7 0.6 reshape.31.picks
  4.3 0.6 fusion.7.place
  4.9 0.0 copy-start.2
  4.9 0.0 copy-start.3
  4.9 13.5 %upward.1 = (bf16[4096,128]{1,0:T(8,128)(2,1)}, bf16[4096,128]{1,0:T(8,128)(2,1)}, bf16[4096,128]{1,0:T(8,128)(2,1)}) custom-call(s32[32,128]{1,0:T(8,128)} %reshape.31.picks, s32[8,128]{1,0:T(8,128)} %fusion.7.place, bf16[216,8192]{1,0:T(8,128)(2,1)} %refs_9_.1, bf16[8,216,216]{2,1,0:T(8,128)(2,1)} %w_hbm.1), custom_call_target="tpu_custom_call" | custom-call | flops 10000000000 | bytes 8388608 | tf_op jit(solution)/shard_map/upward/pallas_call | solution.py:110
  18.4 4.5 %collective-permute-start.6 = (bf16[4096,128]{1,0:T(8,128)(2,1)}, bf16[4096,128]{1,0:T(8,128)(2,1)}, u32[]{:S(2)}, u32[]{:S(2)}) collective-permute-start(bf16[4096,128]{1,0:T(8,128)(2,1)} %get-tuple-element.5), channel_id=1, source_target_pairs={{0,4},{4,8},{8,12},{12,16},{16,20},{20,24},{24,28},{28,32},{32,36}... | collective-permute-start | bytes 3145736 | tf_op jit(solution)/shard_map/ppermute | solution.py:231
  23.0 2.9 %collective-permute-start.7 = (bf16[4096,128]{1,0:T(8,128)(2,1)}, bf16[4096,128]{1,0:T(8,128)(2,1)}, u32[]{:S(2)}, u32[]{:S(2)}) collective-permute-start(bf16[4096,128]{1,0:T(8,128)(2,1)} %get-tuple-element.6), channel_id=1, source_target_pairs={{4,0},{8,4},{12,8},{16,12},{20,16},{24,20},{28,24},{32,28},{36,32}... | collective-permute-start | bytes 3145736 | tf_op jit(solution)/shard_map/ppermute | solution.py:231
  25.9 0.0 copy-done.2
  25.9 0.0 copy-done.3
  26.0 0.4 collective-permute-start.2
  26.3 2.6 %collective-permute-start.1 = (bf16[4,216,216]{2,1,0:T(8,128)(2,1)S(1)}, bf16[4,216,216]{2,1,0:T(8,128)(2,1)S(1)}, u32[]{:S(2)}, u32[]{:S(2)}) collective-permute-start(bf16[4,216,216]{2,1,0:T(8,128)(2,1)S(1)} %broadcast_select_fusion), channel_id=1, source_target_pairs={{2,0},{3,1},{0,2},{1,3},{6,4},{7,5},{4,6},{5,7},{10,8},{11,9},{8,1... | collective-permute-start | bytes 1119752 | tf_op jit(solution)/shard_map/ppermute | solution.py:236
  29.0 1.1 %collective-permute-start = (bf16[4,216,216]{2,1,0:T(8,128)(2,1)S(1)}, bf16[4,216,216]{2,1,0:T(8,128)(2,1)S(1)}, u32[]{:S(2)}, u32[]{:S(2)}) collective-permute-start(bf16[4,216,216]{2,1,0:T(8,128)(2,1)S(1)} %broadcast_select_fusion), channel_id=1, source_target_pairs={{1,0},{2,1},{3,2},{0,3},{5,4},{6,5},{7,6},{4,7},{9,8},{10,9},{11,1... | collective-permute-start | bytes 1119752 | tf_op jit(solution)/shard_map/ppermute | solution.py:236
  30.0 13.8 %all-to-all-start = ((bf16[64,64,128]{2,1,0:T(8,128)(2,1)}), bf16[64,64,128]{2,1,0:T(8,128)(2,1)S(1)}, u32[]{:S(2)}, u32[]{:S(2)}) async-start(bf16[64,64,128]{2,1,0:T(8,128)(2,1)} %bitcast.10), calls=%async_computation | async-start | bytes 2097152 | tf_op jit(solution)/shard_map/all_to_all | solution.py:276
  43.9 0.8 dynamic-slice_multiply_fusion.1
  44.7 0.6 reshape_transpose_reshape.3.src_ref
  45.3 0.0 collective-permute-done.2.refs_3_
  45.3 0.5 collective-permute-start.5
  45.7 2.9 %collective-permute-done.1.refs_2_ = bf16[4,216,216]{2,1,0:T(8,128)(2,1)S(1)} collective-permute-done((bf16[4,216,216]{2,1,0:T(8,128)(2,1)S(1)}, bf16[4,216,216]{2,1,0:T(8,128)(2,1)S(1)}, u32[]{:S(2)}, u32[]{:S(2)}) %collective-permute-start.1) | collective-permute-done | bytes 373280 | tf_op jit(solution)/shard_map/ppermute | solution.py:236
  48.7 0.0 copy-start.5
  48.7 0.0 collective-permute-start.4
  48.7 0.7 collective-permute-done.refs_1_
  49.4 0.0 copy-start.6
  49.4 0.5 collective-permute-start.3
  49.9 0.9 dynamic-slice_multiply_fusion
  50.9 0.1 reshape.29
  51.1 0.7 reshape.30.src_ref
  51.7 0.0 collective-permute-done.5.refs_6_
  51.7 0.0 collective-permute-done.4.refs_5_
  51.7 0.0 collective-permute-done.3.refs_4_
  51.7 0.0 copy-start.8
  51.7 0.0 collective-permute-done.6.refs_7_
  51.8 0.0 collective-permute-done.7.refs_8_
  51.8 0.0 copy-done.4
  51.8 0.0 copy-done.5
  51.8 0.0 copy-done.6
  51.8 0.7 copy-done.7
  52.5 0.1 copy-done.8
  52.6 32.3 %fine.1 = f32[216,2048]{1,0:T(8,128)} custom-call(s32[1]{0:T(128)} %bitcast.core, s32[256,128]{1,0:T(8,128)} %reshape.30.src_ref, bf16[4,216,216]{2,1,0:T(8,128)(2,1)} %refs_0_.2, bf16[4,216,216]{2,1,0:T(8,128)(2,1)} %copy-done.6, bf16[4,216,216]{2,1,0:T(8,128)(2,1)} %copy-done.5, bf16[4,216,216]{2,1,0:T(8,128)(2,1)} %copy-done.4, ...), custom_call_target="tpu_custom_call" | custom-call | flops 20000000000 | bytes 10485760 | tf_op jit(solution)/shard_map/fine/pallas_call | solution.py:204
  84.9 0.0 all-to-all-done
  84.9 0.0 copy-start.1
  85.0 1.0 %copy-done.1 = bf16[64,64,128]{2,1,0:T(8,128)(2,1)} copy-done((bf16[64,64,128]{2,1,0:T(8,128)(2,1)}, bf16[64,64,128]{2,1,0:T(8,128)(2,1)S(1)}, u32[]{:S(2)}) %copy-start.1) | copy-done | bytes 1048600
  85.9 10.2 %coarse.1 = f32[216,512]{1,0:T(8,128)} custom-call(s32[1]{0:T(128)} %bitcast.core, s32[64,128]{1,0:T(8,128)} %reshape_transpose_reshape.3.src_ref, bf16[4,216,216]{2,1,0:T(8,128)(2,1)} %refs_0_.3, bf16[4,216,216]{2,1,0:T(8,128)(2,1)} %copy-done.6, bf16[4,216,216]{2,1,0:T(8,128)(2,1)} %copy-done.5, bf16[4,216,216]{2,1,0:T(8,128)(2,1)} %copy-done.4, ...), custom_call_target="tpu_custom_call" | custom-call | flops 6000000000 | bytes 10485760 | tf_op jit(solution)/shard_map/coarse/pallas_call | solution.py:204
  (6 shorter events, 0.2 us)
Async XLA Ops:
  0.6 2.1 %copy-start = (s32[2,64]{1,0:T(2,128)S(1)}, s32[2,64]{1,0:T(2,128)}, u32[]{:S(2)}) copy-start(s32[2,64]{1,0:T(2,128)} %param.15) | copy-start | bytes 1540
  4.9 21.0 %copy-start.2 = (bf16[4,216,216]{2,1,0:T(8,128)(2,1)S(1)}, bf16[4,216,216]{2,1,0:T(8,128)(2,1)}, u32[]{:S(2)}) copy-start(bf16[4,216,216]{2,1,0:T(8,128)(2,1)} %refs_0_.2) | copy-start | bytes 1119748
  4.9 21.0 %copy-start.3 = (bf16[4,216,216]{2,1,0:T(8,128)(2,1)S(1)}, bf16[4,216,216]{2,1,0:T(8,128)(2,1)}, u32[]{:S(2)}) copy-start(bf16[4,216,216]{2,1,0:T(8,128)(2,1)} %refs_0_.3) | copy-start | bytes 1119748
  18.4 33.3 %collective-permute-start.6 = (bf16[4096,128]{1,0:T(8,128)(2,1)}, bf16[4096,128]{1,0:T(8,128)(2,1)}, u32[]{:S(2)}, u32[]{:S(2)}) collective-permute-start(bf16[4096,128]{1,0:T(8,128)(2,1)} %get-tuple-element.5), channel_id=1, source_target_pairs={{0,4},{4,8},{8,12},{12,16},{16,20},{20,24},{24,28},{28,32},{32,36}... | collective-permute-start | bytes 3145736 | tf_op jit(solution)/shard_map/ppermute | solution.py:231
  23.0 28.8 %collective-permute-start.7 = (bf16[4096,128]{1,0:T(8,128)(2,1)}, bf16[4096,128]{1,0:T(8,128)(2,1)}, u32[]{:S(2)}, u32[]{:S(2)}) collective-permute-start(bf16[4096,128]{1,0:T(8,128)(2,1)} %get-tuple-element.6), channel_id=1, source_target_pairs={{4,0},{8,4},{12,8},{16,12},{20,16},{24,20},{28,24},{32,28},{36,32}... | collective-permute-start | bytes 3145736 | tf_op jit(solution)/shard_map/ppermute | solution.py:231
  26.0 19.3 %collective-permute-start.2 = (bf16[4,216,216]{2,1,0:T(8,128)(2,1)S(1)}, bf16[4,216,216]{2,1,0:T(8,128)(2,1)S(1)}, u32[]{:S(2)}, u32[]{:S(2)}) collective-permute-start(bf16[4,216,216]{2,1,0:T(8,128)(2,1)S(1)} %broadcast_select_fusion), channel_id=1, source_target_pairs={{3,0},{0,1},{1,2},{2,3},{7,4},{4,5},{5,6},{6,7},{11,8},{8,9},{9,10... | collective-permute-start | bytes 1119752 | tf_op jit(solution)/shard_map/ppermute | solution.py:236
  26.3 22.3 %collective-permute-start.1 = (bf16[4,216,216]{2,1,0:T(8,128)(2,1)S(1)}, bf16[4,216,216]{2,1,0:T(8,128)(2,1)S(1)}, u32[]{:S(2)}, u32[]{:S(2)}) collective-permute-start(bf16[4,216,216]{2,1,0:T(8,128)(2,1)S(1)} %broadcast_select_fusion), channel_id=1, source_target_pairs={{2,0},{3,1},{0,2},{1,3},{6,4},{7,5},{4,6},{5,7},{10,8},{11,9},{8,1... | collective-permute-start | bytes 1119752 | tf_op jit(solution)/shard_map/ppermute | solution.py:236
  29.0 20.4 %collective-permute-start = (bf16[4,216,216]{2,1,0:T(8,128)(2,1)S(1)}, bf16[4,216,216]{2,1,0:T(8,128)(2,1)S(1)}, u32[]{:S(2)}, u32[]{:S(2)}) collective-permute-start(bf16[4,216,216]{2,1,0:T(8,128)(2,1)S(1)} %broadcast_select_fusion), channel_id=1, source_target_pairs={{1,0},{2,1},{3,2},{0,3},{5,4},{6,5},{7,6},{4,7},{9,8},{10,9},{11,1... | collective-permute-start | bytes 1119752 | tf_op jit(solution)/shard_map/ppermute | solution.py:236
  30.0 54.9 %all-to-all-start = ((bf16[64,64,128]{2,1,0:T(8,128)(2,1)}), bf16[64,64,128]{2,1,0:T(8,128)(2,1)S(1)}, u32[]{:S(2)}, u32[]{:S(2)}) async-start(bf16[64,64,128]{2,1,0:T(8,128)(2,1)} %bitcast.10), calls=%async_computation | async-start | bytes 2097152 | tf_op jit(solution)/shard_map/all_to_all | solution.py:276
  45.3 6.5 %copy-start.4 = (bf16[4,216,216]{2,1,0:T(8,128)(2,1)}, bf16[4,216,216]{2,1,0:T(8,128)(2,1)S(1)}, u32[]{:S(2)}) copy-start(bf16[4,216,216]{2,1,0:T(8,128)(2,1)S(1)} %collective-permute-done.2.refs_3_) | copy-start | bytes 1119748
  45.3 6.4 %collective-permute-start.5 = (bf16[4,216,216]{2,1,0:T(8,128)(2,1)S(1)}, bf16[4,216,216]{2,1,0:T(8,128)(2,1)S(1)}, u32[]{:S(2)}, u32[]{:S(2)}) collective-permute-start(bf16[4,216,216]{2,1,0:T(8,128)(2,1)S(1)} %collective-permute-done.2.refs_3_), channel_id=1, source_target_pairs={{4,0},{0,4},{12,8},{8,12},{20,16},{16,20},{28,24},{24,28},{36,32},... | collective-permute-start | bytes 1119752 | tf_op jit(solution)/shard_map/ppermute | solution.py:240
  48.7 3.1 %copy-start.5 = (bf16[4,216,216]{2,1,0:T(8,128)(2,1)}, bf16[4,216,216]{2,1,0:T(8,128)(2,1)S(1)}, u32[]{:S(2)}) copy-start(bf16[4,216,216]{2,1,0:T(8,128)(2,1)S(1)} %collective-permute-done.1.refs_2_) | copy-start | bytes 1119748
  48.7 3.0 %collective-permute-start.4 = (bf16[4,216,216]{2,1,0:T(8,128)(2,1)S(1)}, bf16[4,216,216]{2,1,0:T(8,128)(2,1)}, u32[]{:S(2)}, u32[]{:S(2)}) collective-permute-start(bf16[4,216,216]{2,1,0:T(8,128)(2,1)S(1)} %collective-permute-done.1.refs_2_), channel_id=1, source_target_pairs={{4,0},{0,4},{12,8},{8,12},{20,16},{16,20},{28,24},{24,28},{36,32},... | collective-permute-start | bytes 1119752 | tf_op jit(solution)/shard_map/ppermute | solution.py:240
  49.4 2.4 %copy-start.6 = (bf16[4,216,216]{2,1,0:T(8,128)(2,1)}, bf16[4,216,216]{2,1,0:T(8,128)(2,1)S(1)}, u32[]{:S(2)}) copy-start(bf16[4,216,216]{2,1,0:T(8,128)(2,1)S(1)} %collective-permute-done.refs_1_) | copy-start | bytes 1119748
  49.4 2.3 %collective-permute-start.3 = (bf16[4,216,216]{2,1,0:T(8,128)(2,1)S(1)}, bf16[4,216,216]{2,1,0:T(8,128)(2,1)S(1)}, u32[]{:S(2)}, u32[]{:S(2)}) collective-permute-start(bf16[4,216,216]{2,1,0:T(8,128)(2,1)S(1)} %collective-permute-done.refs_1_), channel_id=1, source_target_pairs={{4,0},{0,4},{12,8},{8,12},{20,16},{16,20},{28,24},{24,28},{36,32},... | collective-permute-start | bytes 1119752 | tf_op jit(solution)/shard_map/ppermute | solution.py:240
  51.7 0.8 copy-start.7
  51.7 0.9 copy-start.8
  84.9 1.0 %copy-start.1 = (bf16[64,64,128]{2,1,0:T(8,128)(2,1)}, bf16[64,64,128]{2,1,0:T(8,128)(2,1)S(1)}, u32[]{:S(2)}) copy-start(bf16[64,64,128]{2,1,0:T(8,128)(2,1)S(1)} %all-to-all-done) | copy-start | bytes 3145732
